TPU v7x, 32 devices: a whole 2x2x4 slice. The times are simulated.
32 devices in a mesh: shot: 8 (over z, x), rcv: 2 (over y), surf: 2 (over core).
Axes of the slice: x: 2, y: 2, z: 4, core: 2. Of those that a mesh axis runs over, the one named last changes fastest.
Arguments:
- traces: bfloat16 [2, 8192, 256], P('surf', 'shot'), may hold values from -6 to 6
- trace_block: int32 [2, 8192, 1], P('surf', 'shot'), may hold values from 0 to 7; in each aligned block of 512 rows (0 to 511, 512 to 1023, ..., all dimensions but the last counted through in order) at most 128 rows name the same one
- trace_shot: int32 [2, 8192], P('surf', 'shot'), may hold values from 0 to 15
- trace_point: int32 [2, 8192], P('surf', 'shot'), may hold values from 0 to 255
- recv_panel: bfloat16 [129, 2, 512, 256], P(None, None, ('shot', 'surf'), 'rcv'), may hold values from -0.375 to 0.375
Outputs:
- multiples: bfloat16 [129, 2, 128, 256], P(None, None, ('shot', 'surf'), 'rcv')
Inputs may be any that keep to these rules, and one draw needn't show every extreme that they name: `trace_block`: in each aligned block of 512 rows, at most 128 rows name one shot block.
All inputs are finite; a program needn't handle non-finite values.
Results may differ from a plain program's by a relative error of at most 0.012.
Values may be sent and summed in bfloat16 or wider, within the bound.
No kernel may reach another device: no remote copies, remote signals or barrier semaphores. Data moves between devices by JAX's collectives and lax.ppermute only.
A program may use at most 64 MiB of HBM per device.

v0:
```python
import math

import jax
import jax.numpy as jnp
from jax import lax
from jax.sharding import PartitionSpec as P

SHOTS_PER_INDEX = 16


def transform_rows(samples, window_len, bin_count):
    sample_index = lax.broadcasted_iota(jnp.int32, (window_len, bin_count), 0)
    freq_index = lax.broadcasted_iota(jnp.int32, (window_len, bin_count), 1)
    phase_angle = (sample_index * freq_index % window_len).astype(jnp.float32) * (
        2.0 * math.pi / window_len
    )
    norm_factor = 1.0 / math.sqrt(window_len)
    table = jnp.concatenate(
        [jnp.cos(phase_angle) * norm_factor, -jnp.sin(phase_angle) * norm_factor], axis=1
    )
    table_high = table.astype(jnp.bfloat16)
    table_low = (table - table_high.astype(jnp.float32)).astype(jnp.bfloat16)
    result = jnp.dot(samples, table_high, preferred_element_type=jnp.float32)
    result = result + jnp.dot(samples, table_low, preferred_element_type=jnp.float32)
    real_part = result[:, :bin_count]
    imag_part = result[:, bin_count:]
    return jnp.stack([real_part, imag_part], axis=1).astype(jnp.bfloat16)


def route_rows(spectra, owners, targets, places, owner_count, empty_id):
    row_count = owners.shape[0]
    owner_hit = owners[:, None] == lax.broadcasted_iota(jnp.int32, (1, owner_count), 1)
    earlier = lax.broadcasted_iota(jnp.int32, (row_count, row_count), 0) > lax.broadcasted_iota(
        jnp.int32, (row_count, row_count), 1
    )
    before = jnp.dot(
        earlier.astype(jnp.bfloat16),
        owner_hit.astype(jnp.bfloat16),
        preferred_element_type=jnp.float32,
    )
    slot_rank = jnp.sum(jnp.where(owner_hit, before, 0.0), axis=1).astype(jnp.int32)
    position = owners * places + slot_rank
    slot_total = owner_count * places
    slot_hit = position[:, None] == lax.broadcasted_iota(jnp.int32, (1, slot_total), 1)
    flat_spectra = spectra.reshape(row_count, -1)
    buffer = lax.dot_general(
        slot_hit.astype(jnp.bfloat16),
        flat_spectra,
        (((0,), (0,)), ((), ())),
        preferred_element_type=jnp.float32,
    )
    buffer = buffer.astype(spectra.dtype)
    labels = jnp.max(jnp.where(slot_hit, targets[:, None], -1), axis=0)
    labels = jnp.where(labels < 0, empty_id, labels)
    return (
        buffer.reshape((owner_count, places) + spectra.shape[1:]),
        labels.reshape(owner_count, places),
    )


def bin_panel(received, labels, shot_rows, point_count):
    freq_count = received.shape[-1]
    flat_rows = received.reshape(-1, 2 * freq_count)
    flat_labels = labels.reshape(-1)
    point_iota = lax.broadcasted_iota(jnp.int32, (1, point_count), 1)

    def one_shot(shot_id):
        local_label = flat_labels - shot_id * point_count
        point_hit = local_label[:, None] == point_iota
        totals = lax.dot_general(
            point_hit.astype(jnp.bfloat16),
            flat_rows,
            (((0,), (0,)), ((), ())),
            preferred_element_type=jnp.float32,
        )
        coverage = jnp.sum(point_hit.astype(jnp.float32), axis=0)
        return (totals / jnp.maximum(coverage, 1.0)[:, None]).astype(jnp.bfloat16)

    panel = lax.map(one_shot, jnp.arange(shot_rows, dtype=jnp.int32))
    return panel.reshape(shot_rows, point_count, 2, freq_count).transpose(3, 2, 0, 1)


def product(left_edge, right_edge):
    return jnp.einsum("bhv,bvy->bhy", left_edge, right_edge, preferred_element_type=jnp.float32)


def local(traces, trace_block, trace_shot, trace_point, recv_panel):
    shot_count = lax.axis_size("shot")
    rcv_count = lax.axis_size("rcv")
    freq_count = recv_panel.shape[0]
    half_points = recv_panel.shape[2] * shot_count
    window_len = traces.shape[2]
    row_count = traces.shape[1]
    part_rows = row_count // rcv_count
    capacity = 2 * part_rows // shot_count
    empty_id = SHOTS_PER_INDEX * half_points
    samples = traces[0]
    owners = trace_block[0, :, 0]
    targets = trace_shot[0] * half_points + trace_point[0]
    spectra = transform_rows(samples, window_len, freq_count)
    buffer, labels = route_rows(
        spectra, owners, targets, rcv_count * capacity, shot_count, empty_id
    )
    received, got_labels = (
        lax.all_to_all(buffer, "shot", split_axis=0, concat_axis=0, tiled=True),
        lax.all_to_all(labels, "shot", split_axis=0, concat_axis=0, tiled=True),
    )
    panel = bin_panel(received, got_labels, SHOTS_PER_INDEX, half_points)
    receiver = lax.all_gather(recv_panel, "shot", axis=2, tiled=True)
    real_part = product(panel[:, 0], receiver[:, 0]) - product(panel[:, 1], receiver[:, 1])
    imag_part = product(panel[:, 0], receiver[:, 1]) + product(panel[:, 1], receiver[:, 0])
    partial_value = jnp.stack([real_part, imag_part], axis=1)
    half_term = lax.optimization_barrier(partial_value.astype(jnp.bfloat16)).astype(jnp.float32)
    result = lax.psum_scatter(
        half_term.astype(jnp.bfloat16), "surf", scatter_dimension=2, tiled=True
    )
    return result


def solution(mesh):
    in_specs = (
        P("surf", "shot", None),
        P("surf", "shot", None),
        P("surf", "shot"),
        P("surf", "shot"),
        P(None, None, ("shot", "surf"), "rcv"),
    )
    out_specs = P(None, None, ("shot", "surf"), "rcv")
    return jax.shard_map(local, mesh=mesh, in_specs=in_specs, out_specs=out_specs, check_vma=False)
```

profile of v0, /device:TPU:0, one launch (start us, length us, event | category | flops | bytes accessed | tf_op | source)
XLA Modules:
  0.0 382.5 jit_solution(8671845005390449973)
XLA Ops:
  6.5 3.4 copy.36
  9.9 0.6 negate_multiply_fusion
  11.5 0.4 copy-done.3
  11.9 0.5 fusion.27
  12.4 1.8 fusion.17
  14.6 1.8 copy.32
  16.4 7.3 %all-to-all-start.1 = ((bf16[8,256,2,129]{1,2,3,0:T(2,128)(2,1)}), bf16[8,256,2,129]{1,2,3,0:T(2,128)(2,1)S(1)}, u32[]{:S(2)}, u32[]{:S(2)}) async-start(bf16[8,256,2,129]{1,2,3,0:T(2,128)(2,1)} %copy.32), calls=%async_computation.1 | async-start | bytes 2113536 | tf_op jit(solution)/shard_map/all_to_all | solution.py:105
  23.7 1.6 select_reduce_fusion
  25.3 0.6 compare_select_fusion
  25.9 35.4 %all-to-all-done.1 = bf16[8,256,2,129]{1,2,3,0:T(2,128)(2,1)S(1)} async-done(((bf16[8,256,2,129]{1,2,3,0:T(2,128)(2,1)}), bf16[8,256,2,129]{1,2,3,0:T(2,128)(2,1)S(1)}, u32[]{:S(2)}, u32[]{:S(2)}) %all-to-all-start.1) | async-done | bytes 1056800 | tf_op jit(solution)/shard_map/all_to_all | solution.py:105
  61.3 15.1 %all-to-all-start = ((s32[8,1,256]{2,1,0:T(1,128)}), s32[8,1,256]{2,1,0:T(1,128)S(1)}, u32[]{:S(2)}, u32[]{:S(2)}) async-start(s32[8,1,256]{2,1,0:T(1,128)} %compare_select_fusion), calls=%async_computation | async-start | bytes 16384 | tf_op jit(solution)/shard_map/all_to_all | solution.py:106
  76.7 8.1 %copy.38 = bf16[8,256,2,129]{3,2,1,0:T(2,128)(2,1)S(1)} copy(bf16[8,256,2,129]{1,2,3,0:T(2,128)(2,1)} %copy-done.2) | data formatting | bytes 2113536
  84.7 2.0 reshape.74
  86.8 74.5 %while.11 = (s32[]{:T(128)}, bf16[16,256,258]{1,2,0:T(8,128)(2,1)}, s32[16]{0:T(128)S(1)}, s32[2048]{0:T(1024)S(1)}, bf16[2048,258]{1,0:T(8,128)(2,1)}, /*index=5*/s32[]{:T(128)}, s32[1]{0:T(128)}) while((s32[]{:T(128)}, bf16[16,256,258]{1,2,0:T(8,128)(2,1)}, s32[16]{0:T(128)S(1)}, s32[2048]{0:T(1024)S(1)}, ...), condition=%wide.region_4.5_spmd.clone, body=%wide.region_2.4_spmd.clone.sunk | while | flops 272763904 | bytes 1745513 | solution.py:79
  86.8 0.6 dynamic_slice.6
  88.0 0.4 fusion.48
  88.4 3.0 fusion.49
  91.4 0.6 dynamic_slice.6
  93.0 3.0 fusion.49
  96.1 0.6 dynamic_slice.6
  97.3 0.4 fusion.48
  97.7 3.1 fusion.49
  100.7 0.6 dynamic_slice.6
  102.3 3.0 fusion.49
  105.4 0.6 dynamic_slice.6
  106.6 0.4 fusion.48
  107.0 3.1 fusion.49
  110.1 0.6 dynamic_slice.6
  111.7 3.0 fusion.49
  114.7 0.6 dynamic_slice.6
  116.0 0.4 fusion.48
  116.3 3.0 fusion.49
  119.4 0.6 dynamic_slice.6
  120.6 0.4 fusion.48
  121.0 3.1 fusion.49
  124.0 0.6 dynamic_slice.6
  125.6 3.1 fusion.49
  128.7 0.6 dynamic_slice.6
  129.9 0.4 fusion.48
  130.3 3.1 fusion.49
  133.3 0.6 dynamic_slice.6
  134.6 0.4 fusion.48
  135.0 3.1 fusion.49
  138.0 0.6 dynamic_slice.6
  139.6 3.0 fusion.49
  142.7 0.6 dynamic_slice.6
  144.3 3.0 fusion.49
  147.3 0.6 dynamic_slice.6
  148.9 3.0 fusion.49
  152.0 0.6 dynamic_slice.6
  153.6 3.1 fusion.49
  156.6 0.6 dynamic_slice.6
  158.2 3.0 fusion.49
  161.3 2.0 copy.35
  163.3 186.5 %all-gather.2.cloned.1.call-done = bf16[129,2,256,128]{3,2,0,1:T(8,128)(2,1)} async-done(((bf16[129,2,32,128]{3,2,0,1:T(8,128)(2,1)}), bf16[129,2,256,128]{3,2,0,1:T(8,128)(2,1)}) %all-gather.2.cloned.1.call-update) | async-done | bytes 16908304 | tf_op jit(solution)/shard_map/all_gather | solution.py:109
  349.8 4.8 %fusion.12 = f32[129,16,128]{2,1,0:T(8,128)S(1)} fusion(bf16[129,2,256,128]{3,2,0,1:T(8,128)(2,1)} %all-gather.2.cloned.1.call-done, bf16[129,2,16,256]{3,2,0,1:T(8,128)(2,1)S(1)} %bitcast.76), kind=kOutput, calls=%fused_computation.18 | convolution fusion | flops 135266304 | bytes 10567680 | tf_op jit(solution)/shard_map/bhv,bvy->bhy/dot_general | solution.py:84
  354.5 5.4 %fusion.11 = f32[129,16,128]{2,1,0:T(8,128)S(1)} fusion(bf16[129,2,256,128]{3,2,0,1:T(8,128)(2,1)} %all-gather.2.cloned.1.call-done, bf16[129,2,16,256]{3,2,0,1:T(8,128)(2,1)S(1)} %bitcast.77), kind=kOutput, calls=%fused_computation.17 | convolution fusion | flops 135266304 | bytes 10567680 | tf_op jit(solution)/shard_map/bhv,bvy->bhy/dot_general | solution.py:84
  359.9 0.5 copy-done.1
  360.4 1.3 fusion.24
  361.7 1.3 fusion.25
  363.4 1.3 reshape.75
  364.7 8.7 %reduce-scatter.4.cloned.1.call-done = bf16[8,33024]{1,0:T(8,128)(2,1)} async-done(((bf16[16,33024]{1,0:T(8,128)(2,1)}), bf16[8,33024]{1,0:T(8,128)(2,1)}) %reduce-scatter.4.cloned.1.call-update) | async-done | bytes 528400
  373.4 1.3 reshape.76
  374.7 0.9 copy.37
  (69 shorter events, 5.3 us)
Async XLA Ops:
  6.5 4.0 %copy-start = (bf16[1,1024,256]{2,1,0:T(8,128)(2,1)S(1)}, bf16[1,1024,256]{2,1,0:T(8,128)(2,1)}, u32[]{:S(2)}) copy-start(bf16[1,1024,256]{2,1,0:T(8,128)(2,1)} %param.7) | copy-start | bytes 1572868
  6.5 343.2 %all-gather.2.cloned.1.call-start = ((), (), s32[]{:S(2)}) async-start(), calls=%async_computation.3 | async-start | bytes 19021824 | tf_op jit(solution)/shard_map/all_gather | solution.py:109
  11.2 0.7 copy-start.3
  14.6 9.1 %copy-start.4 = (s32[1,1024]{1,0:T(1,128)S(1)}, s32[1,1024]{1,0:T(1,128)}, u32[]{:S(2)}) copy-start(s32[1,1024]{1,0:T(1,128)} %param.10) | copy-start | bytes 12292
  14.6 9.1 %copy-start.5 = (s32[1,1024]{1,0:T(1,128)S(1)}, s32[1,1024]{1,0:T(1,128)}, u32[]{:S(2)}) copy-start(s32[1,1024]{1,0:T(1,128)} %param.9) | copy-start | bytes 12292
  16.4 44.9 %all-to-all-start.1 = ((bf16[8,256,2,129]{1,2,3,0:T(2,128)(2,1)}), bf16[8,256,2,129]{1,2,3,0:T(2,128)(2,1)S(1)}, u32[]{:S(2)}, u32[]{:S(2)}) async-start(bf16[8,256,2,129]{1,2,3,0:T(2,128)(2,1)} %copy.32), calls=%async_computation.1 | async-start | bytes 2113536 | tf_op jit(solution)/shard_map/all_to_all | solution.py:105
  61.3 15.3 %copy-start.2 = (bf16[8,256,2,129]{1,2,3,0:T(2,128)(2,1)}, bf16[8,256,2,129]{1,2,3,0:T(2,128)(2,1)S(1)}, u32[]{:S(2)}) copy-start(bf16[8,256,2,129]{1,2,3,0:T(2,128)(2,1)S(1)} %all-to-all-done.1) | copy-start | bytes 3170308
  61.3 25.5 %all-to-all-start = ((s32[8,1,256]{2,1,0:T(1,128)}), s32[8,1,256]{2,1,0:T(1,128)S(1)}, u32[]{:S(2)}, u32[]{:S(2)}) async-start(s32[8,1,256]{2,1,0:T(1,128)} %compare_select_fusion), calls=%async_computation | async-start | bytes 16384 | tf_op jit(solution)/shard_map/all_to_all | solution.py:106
  76.4 297.0 %reduce-scatter.4.cloned.1.call-start = ((), (), s32[]{:S(2)}) async-start(), calls=%async_computation.4 | async-start | bytes 1585152
  349.8 10.6 %copy-start.1 = (bf16[129,2,256,128]{3,2,0,1:T(8,128)(2,1)S(1)}, bf16[129,2,256,128]{3,2,0,1:T(8,128)(2,1)}, u32[]{:S(2)}) copy-start(bf16[129,2,256,128]{3,2,0,1:T(8,128)(2,1)} %all-gather.2.cloned.1.call-done) | copy-start | bytes 50724868
Sparse Core Ops, SparseCore 0:
  10.0 339.6 all-gather.1
  364.8 8.5 reduce-scatter.3
where the time goes:
time: 384 us; the launch traced here: 382 us
  waiting for transfers between devices  231 us (60%)
  matrix products  64.5 us (17%)
  local copies, waits for them, and re-layouts  31.9 us (8%)
  starting transfers between devices  22.6 us (6%)
  between operations  13.6 us (4%)
  loops' own time  10.6 us (3%)
  other arithmetic  8.76 us (2%)
    all_gather x1, waiting for transfers between devices, local(): receiver = lax.all_gather(recv_panel, 'shot', axis=2, tiled=True)  186 us
    dot_general x16, matrix products, one_shot(): lax.dot_general(point_hit.astype(jnp.bfloat16), flat_rows, (((0,), (0,)),...  48.8 us
    all_to_all x1, waiting for transfers between devices, local(): lax.all_to_all(buffer, 'shot', split_axis=0, concat_axis=0, tiled=True)  35.4 us
    unnamed x20, local copies, waits for them, and re-layouts  17.6 us
    all_to_all x1, starting transfers between devices, local(): lax.all_to_all(labels, 'shot', split_axis=0, concat_axis=0, tiled=True)  15.1 us
    dot_general x4, matrix products, product(): jnp.einsum('bhv,bvy->bhy', left_edge, right_edge, preferred_element_type=...  12.7 us
    another operation x1, loops' own time, bin_panel(): panel = lax.map(one_shot, jnp.arange(shot_rows, dtype=jnp.int32))  10.6 us
    dynamic_slice x16, local copies, waits for them, and re-layouts, bin_panel(): panel = lax.map(one_shot, jnp.arange(shot_rows, dtype=jnp.int32))  9.32 us
  transfers between devices with their start and end apart: 4, of which 3 were waited for; matrix products, arithmetic and copies ran while one was open for 22% of the time, Pallas kernels for 0%

commit v1 on v0

v1 whole, which is shorter than its diff:
```python
import functools
import math

import jax
import jax.numpy as jnp
import numpy as np
from jax import lax
from jax.experimental import pallas as pl
from jax.experimental.pallas import tpu as pltpu
from jax.sharding import PartitionSpec as P

SHOTS_PER_INDEX = 16
VMEM = pl.BlockSpec(memory_space=pltpu.VMEM)
SMEM = pl.BlockSpec(memory_space=pltpu.SMEM)
LIMIT = 56 * 1024 * 1024


def dft_tables(window, groups, width, top):
    slots = -(-(2 * width + 4) // 16) * 16
    n = np.arange(window, dtype=np.int64)
    table = np.zeros((groups, slots, window), np.float64)
    for g in range(groups):
        freqs = list(range(g * width, (g + 1) * width)) + [top]
        for j, f in enumerate(freqs):
            angle = (n * f % window) * (2.0 * math.pi / window)
            table[g, 2 * j] = np.cos(angle)
            table[g, 2 * j + 1] = -np.sin(angle)
    table = (table / math.sqrt(window)).astype(np.float32)
    high = table.astype(jnp.bfloat16)
    low = (table - high.astype(np.float32)).astype(jnp.bfloat16)
    return high, low, slots


def nt(a, b):
    return lax.dot_general(a, b, (((1,), (1,)), ((), ())), preferred_element_type=jnp.float32)


def spectra_kernel(slots, id_slot, x_ref, high_ref, low_ref, shot_ref, point_ref, out_ref):
    x = x_ref[...]
    y = nt(high_ref[...], x) + nt(low_ref[...], x)
    groups = out_ref.shape[0]
    y = y.reshape(groups, slots, x.shape[0])
    place = lax.broadcasted_iota(jnp.int32, y.shape, 1)
    y = jnp.where(place == id_slot, shot_ref[...].astype(jnp.float32)[None], y)
    y = jnp.where(place == id_slot + 1, point_ref[...].astype(jnp.float32)[None], y)
    out_ref[...] = y.astype(jnp.bfloat16)


def bin_kernel(
    halves, shots, points, cols, id_slot, me_ref, rows_ref, own_ref, panel_ref, top_ref, acc_ref, top_acc_ref
):
    sources = rows_ref.shape[0] // halves
    width = own_ref.shape[1]
    n_rows = rows_ref.shape[2]
    own_shot, own_half = me_ref[0], me_ref[1]

    def hits(source, count, slot, first):
        ids = rows_ref[source, slot : slot + 1, :].astype(jnp.float32) - first
        grid = lax.broadcasted_iota(jnp.int32, (count, n_rows), 0).astype(jnp.float32)
        return jnp.where(grid == ids, 1.0, 0.0).astype(jnp.bfloat16)

    for half in range(halves):

        def step(s, carry):
            source = s * halves + half
            shot_hit = hits(source, shots, id_slot, 0.0)
            point_hit = hits(source, points, id_slot + 1, 0.0)
            for c in range(cols + 1):
                left = shot_hit if c == cols else shot_hit * rows_ref[source, c : c + 1, :]
                got = nt(left, point_hit)
                acc_ref[c] = jnp.where(s == 0, got, acc_ref[c] + got)
            return carry

        lax.fori_loop(0, sources, step, 0)
        scale = 1.0 / jnp.maximum(acc_ref[cols], 1.0)
        for c in range(cols):
            panel_ref[c, :, half * points : (half + 1) * points] = (acc_ref[c] * scale).astype(jnp.bfloat16)

    def top_step(s, carry):
        source = s * halves + own_half
        shot_hit = hits(source, shots, id_slot, 0.0)
        point_hit = hits(source, width, id_slot + 1, (own_shot * width).astype(jnp.float32))
        for c in range(3):
            left = shot_hit if c == 2 else shot_hit * rows_ref[source, cols + c : cols + c + 1, :]
            got = nt(left, point_hit)
            top_acc_ref[c] = jnp.where(s == 0, got, top_acc_ref[c] + got)
        return carry

    lax.fori_loop(0, sources, top_step, 0)
    scale = 1.0 / jnp.maximum(top_acc_ref[2], 1.0)
    real = (top_acc_ref[0] * scale).astype(jnp.bfloat16)
    imag = (top_acc_ref[1] * scale).astype(jnp.bfloat16)
    dot = functools.partial(jnp.dot, preferred_element_type=jnp.float32)
    own_real, own_imag = own_ref[0], own_ref[1]
    out_real = dot(real, own_real) - dot(imag, own_imag)
    out_imag = dot(real, own_imag) + dot(imag, own_real)
    targets = top_ref.shape[0]
    block = shots // targets
    for t in range(targets):
        rows = slice(t * block, (t + 1) * block)
        top_ref[t] = jnp.concatenate([out_real[rows], out_imag[rows]], axis=0).astype(jnp.bfloat16)


def product_kernel(n_shot, n_rcv, halves, width, panel_ref, recv_ref, out_ref):
    shots = panel_ref.shape[1]
    left = panel_ref[...].reshape(2 * shots, panel_ref.shape[2])
    sides = []
    for c in range(2):
        blocks = []
        for r in range(n_rcv):
            rows = [
                recv_ref[(s * n_rcv + r) * halves + h, c * width : (c + 1) * width, :]
                for h in range(halves)
                for s in range(n_shot)
            ]
            blocks.append(jnp.concatenate(rows, axis=0))
        right = blocks[0] if n_rcv == 1 else jnp.concatenate(blocks, axis=1)
        sides.append(jnp.dot(left, right, preferred_element_type=jnp.float32))
    real = sides[0][:shots] - sides[1][shots:]
    imag = sides[1][:shots] + sides[0][shots:]
    lanes = recv_ref.shape[2]
    block = shots // (n_shot * halves)
    for s in range(n_shot):
        for h in range(halves):
            first = (s * halves + h) * block
            both = jnp.concatenate([real[first : first + block], imag[first : first + block]], axis=0)
            for r in range(n_rcv):
                out_ref[(s * n_rcv + r) * halves + h] = both[:, r * lanes : (r + 1) * lanes].astype(jnp.bfloat16)


def local(traces, trace_block, trace_shot, trace_point, recv_panel):
    n_shot, n_rcv, halves = lax.axis_size("shot"), lax.axis_size("rcv"), lax.axis_size("surf")
    freqs, _, width, lanes = recv_panel.shape
    window, n_rows = traces.shape[2], traces.shape[1]
    shots, points = SHOTS_PER_INDEX * n_shot, width * n_shot
    assert max(shots, points) <= 256
    main = freqs - 1
    pairs = n_shot * halves
    spread = main % (pairs * n_rcv) == 0
    across = n_rcv if spread else 1
    axes = ("shot", "rcv", "surf") if spread else ("shot", "surf")
    groups = pairs * across
    per = main // groups
    cols = 2 * per
    block = shots // pairs
    high, low, slots = dft_tables(window, groups, per, main)

    def own_table(table):
        table = jnp.asarray(table).reshape(n_shot, across, halves, slots, window)
        table = lax.dynamic_index_in_dim(table, lax.axis_index("rcv") if spread else 0, 1, keepdims=False)
        return table.reshape(pairs * slots, window)

    shot_ids = trace_block.reshape(1, n_rows) * SHOTS_PER_INDEX + trace_shot
    me = jnp.stack([lax.axis_index("shot"), lax.axis_index("surf")]).astype(jnp.int32)

    recv = recv_panel[:main].reshape(groups, per * 2 * width, lanes)
    recv = lax.all_to_all(recv, axes, split_axis=0, concat_axis=0, tiled=True)

    message = pl.pallas_call(
        functools.partial(spectra_kernel, slots, cols + 2),
        out_shape=jax.ShapeDtypeStruct((pairs, slots, n_rows), jnp.bfloat16),
        in_specs=[VMEM] * 5,
        out_specs=VMEM,
        compiler_params=pltpu.CompilerParams(vmem_limit_bytes=LIMIT),
    )(traces[0], own_table(high), own_table(low), shot_ids, trace_point)
    rows = lax.all_to_all(message, ("shot", "surf"), split_axis=0, concat_axis=0, tiled=True)

    panel, top = pl.pallas_call(
        functools.partial(bin_kernel, halves, shots, points, cols, cols + 2),
        out_shape=(
            jax.ShapeDtypeStruct((cols, shots, halves * points), jnp.bfloat16),
            jax.ShapeDtypeStruct((pairs, 2 * block, lanes), jnp.bfloat16),
        ),
        in_specs=[SMEM, VMEM, VMEM],
        out_specs=(VMEM, VMEM),
        scratch_shapes=[
            pltpu.VMEM((cols + 1, shots, points), jnp.float32),
            pltpu.VMEM((3, shots, width), jnp.float32),
        ],
        compiler_params=pltpu.CompilerParams(vmem_limit_bytes=LIMIT),
    )(me, rows, recv_panel[main])
    top = lax.all_to_all(top, ("shot", "surf"), split_axis=0, concat_axis=0, tiled=True)
    top = jnp.sum(top.astype(jnp.float32), axis=0).astype(jnp.bfloat16).reshape(1, 2, block, lanes)

    out = pl.pallas_call(
        functools.partial(product_kernel, n_shot, across, halves, width),
        grid=(per,),
        out_shape=jax.ShapeDtypeStruct((groups, per * 2 * block, lanes), jnp.bfloat16),
        in_specs=[
            pl.BlockSpec((2, shots, halves * points), lambda f: (f, 0, 0)),
            pl.BlockSpec((groups, 2 * width, lanes), lambda f: (0, f, 0)),
        ],
        out_specs=pl.BlockSpec((groups, 2 * block, lanes), lambda f: (0, f, 0)),
        compiler_params=pltpu.CompilerParams(vmem_limit_bytes=LIMIT),
    )(panel, recv)
    out = lax.all_to_all(out, axes, split_axis=0, concat_axis=0, tiled=True)
    return jnp.concatenate([out.reshape(main, 2, block, lanes), top], axis=0)


def solution(mesh):
    in_specs = (
        P("surf", "shot", None),
        P("surf", "shot", None),
        P("surf", "shot"),
        P("surf", "shot"),
        P(None, None, ("shot", "surf"), "rcv"),
    )
    out_specs = P(None, None, ("shot", "surf"), "rcv")
    return jax.shard_map(local, mesh=mesh, in_specs=in_specs, out_specs=out_specs, check_vma=False)
```

time: 384 us -> 112 us (0.29)
  waiting for transfers between devices: 231 us -> 46.2 us
  matrix products: 64.5 us -> 0 us
  Pallas kernels: 0 us -> 38.1 us
  local copies, waits for them, and re-layouts: 31.9 us -> 4.78 us
  between operations: 13.6 us -> 0.07 us
  loops' own time: 10.6 us -> 0 us
  other arithmetic: 8.76 us -> 2.9 us
    all_gather x1 -> x0, waiting for transfers between devices: 186 us -> none  [local(): receiver = lax.all_gather(recv_panel, 'shot', axis=2, tiled=True)]
    dot_general x24 -> x0, matrix products: 64.5 us -> none  [the longest x16 48.8 us: one_shot(): lax.dot_general(point_hit.astype(jnp.bfloat16), flat_rows, (((0,), (0,)),...]
    pallas_call x0 -> x3, Pallas kernels: none -> 38.1 us  [the longest x1 31.5 us: local(): pl.pallas_call(functools.partial(bin_kernel, halves, shots, points, cols,...]
    unnamed x20 -> x6, local copies, waits for them, and re-layouts: 17.6 us -> 0.01 us
    all_to_all x2 -> x4, waiting for transfers between devices: 35.4 us -> 46.2 us  [the longest x1 15.5 us: local(): out = lax.all_to_all(out, axes, split_axis=0, concat_axis=0, tiled=True)]
    another operation x1 -> x0, loops' own time: 10.6 us -> none  [bin_panel(): panel = lax.map(one_shot, jnp.arange(shot_rows, dtype=jnp.int32))]
    unnamed x3 -> x0, waiting for transfers between devices: 8.72 us -> none
    dynamic_slice x16 -> x1, local copies, waits for them, and re-layouts: 9.32 us -> 1.7 us  [own_table(): lax.dynamic_index_in_dim(table, lax.axis_index('rcv') if spread else 0, 1...]
  transfers between devices with their start and end apart: 4 -> 4, of which waited for: 3 -> 4; matrix products, arithmetic and copies ran while one was open for 22% -> 3% of each run, Pallas kernels for 0% -> 32%
where the time goes in v1:
time: 112 us; the launch traced here: 111 us
  waiting for transfers between devices  46.2 us (41%)
  Pallas kernels  38.1 us (34%)
  starting transfers between devices  18.9 us (17%)
  local copies, waits for them, and re-layouts  4.78 us (4%)
  other arithmetic  2.9 us (3%)
    pallas_call x1, Pallas kernels, local(): pl.pallas_call(functools.partial(bin_kernel, halves, shots, points, cols,...  31.5 us
    all_to_all x1, waiting for transfers between devices, local(): out = lax.all_to_all(out, axes, split_axis=0, concat_axis=0, tiled=True)  15.5 us
    all_to_all x1, waiting for transfers between devices, local(): recv = lax.all_to_all(recv, axes, split_axis=0, concat_axis=0, tiled=True)  15.4 us
    all_to_all x1, waiting for transfers between devices, local(): lax.all_to_all(message, ('shot', 'surf'), split_axis=0, concat_axis=0, ti...  12.7 us
    all_to_all x1, starting transfers between devices, local(): lax.all_to_all(message, ('shot', 'surf'), split_axis=0, concat_axis=0, ti...  7.35 us
    pallas_call x1, Pallas kernels, local(): pl.pallas_call(functools.partial(product_kernel, n_shot, across, halves,...  4.24 us
    all_to_all x1, starting transfers between devices, local(): recv = lax.all_to_all(recv, axes, split_axis=0, concat_axis=0, tiled=True)  4.04 us
    all_to_all x1, starting transfers between devices, local(): out = lax.all_to_all(out, axes, split_axis=0, concat_axis=0, tiled=True)  3.79 us
  transfers between devices with their start and end apart: 4, of which 4 were waited for; matrix products, arithmetic and copies ran while one was open for 3% of the time, Pallas kernels for 32%

profile of v1, /device:TPU:0, one launch (start us, length us, event | category | flops | bytes accessed | tf_op | source)
XLA Modules:
  0.0 111.0 jit_solution(2758996068059596468)
XLA Ops:
  0.0 0.0 copy-start.1
  0.0 1.5 %bitcast_add_fusion.shot_ref = s32[1,1024]{1,0:T(1,128)} fusion(s32[1,1024]{1,0:T(1,128)} %param.9, s32[1,1024,1]{1,2,0:T(1,128)} %param.8), kind=kLoop, calls=%fused_computation.2 | loop fusion | flops 2048 | bytes 12288 | tf_op jit(solution)/shard_map/add | solution.py:153
  1.5 1.7 %constant_dynamic-slice_fusion = (bf16[8,1,2,16,256]{4,3,2,0,1:T(8,128)(2,1)}, bf16[8,1,2,16,256]{4,3,2,0,1:T(8,128)(2,1)}) fusion(bf16[8,2,2,16,256]{4,3,2,0,1:T(8,128)(2,1)} %constant.36, s32[]{:T(128)S(6)} %select_n.5, bf16[8,2,2,16,256]{4,3,2,0,1:T(8,128)(2,1)} %constant.35), kind=kLoop, calls=%fused_computation.4 | loop fusion | bytes 524292 | tf_op jit(solution)/shard_map/jit(dynamic_index_in_dim)/dynamic_slice | solution.py:150
  3.2 2.4 %shard_map.73 = bf16[16,16,1024]{2,1,0:T(8,128)(2,1)} custom-call(bf16[1024,256]{1,0:T(8,128)(2,1)} %bitcast.16, bf16[256,256]{1,0:T(8,128)(2,1)} %bitcast.15, bf16[256,256]{1,0:T(8,128)(2,1)} %bitcast.14, s32[1,1024]{1,0:T(1,128)} %bitcast_add_fusion.shot_ref, s32[1,1024]{1,0:T(1,128)} %point_ref.1), custom_call_target="tpu_custom_call" | custom-call | tf_op jit(solution)/shard_map/pallas_call | solution.py:159
  5.6 7.4 %all-to-all-start = ((bf16[16,16,1024]{2,1,0:T(8,128)(2,1)}), bf16[16,16,1024]{2,1,0:T(8,128)(2,1)S(1)}, u32[]{:S(2)}, u32[]{:S(2)}) async-start(bf16[16,16,1024]{2,1,0:T(8,128)(2,1)} %shard_map.73), calls=%async_computation | async-start | bytes 1048576 | tf_op jit(solution)/shard_map/all_to_all | solution.py:166
  12.9 0.0 copy-done.1
  12.9 1.8 %slice.7 = bf16[128,2,32,128]{3,2,1,0:T(8,128)(2,1)} slice(bf16[129,2,32,128]{3,2,1,0:T(8,128)(2,1)S(1)} %copy-done.1), slice={[0:128], [0:2], [0:32], [0:128]} | slice | bytes 4194304 | tf_op jit(solution)/shard_map/slice | solution.py:156
  14.7 12.7 %all-to-all-done.rows_ref = bf16[16,16,1024]{2,1,0:T(8,128)(2,1)S(1)} async-done(((bf16[16,16,1024]{2,1,0:T(8,128)(2,1)}), bf16[16,16,1024]{2,1,0:T(8,128)(2,1)S(1)}, u32[]{:S(2)}, u32[]{:S(2)}) %all-to-all-start) | async-done | bytes 524320 | tf_op jit(solution)/shard_map/all_to_all | solution.py:166
  27.4 0.0 copy-start.2
  27.4 4.0 %all-to-all-start.1 = ((bf16[32,256,128]{2,1,0:T(8,128)(2,1)}), bf16[32,256,128]{2,1,0:T(8,128)(2,1)S(1)}, u32[]{:S(2)}, u32[]{:S(2)}) async-start(bf16[32,256,128]{2,1,0:T(8,128)(2,1)} %bitcast.12), calls=%async_computation.1 | async-start | bytes 4194304 | tf_op jit(solution)/shard_map/all_to_all | solution.py:157
  31.4 0.6 pad_add_fusion.me_ref
  32.0 1.3 %slice_bitcast_fusion.own_ref = bf16[2,32,128]{2,1,0:T(8,128)(2,1)} fusion(bf16[129,2,32,128]{3,2,1,0:T(8,128)(2,1)} %param.11), kind=kLoop, calls=%fused_computation.1 | loop fusion | bytes 32768 | tf_op jit(solution)/shard_map/squeeze | solution.py:181
  33.3 0.0 copy-done.2
  33.3 31.5 %shard_map.74 = (bf16[8,128,512]{2,1,0:T(8,128)(2,1)}, bf16[16,16,128]{2,1,0:T(8,128)(2,1)}) custom-call(s32[2]{0:T(128)} %pad_add_fusion.me_ref, bf16[16,16,1024]{2,1,0:T(8,128)(2,1)} %copy-done.2, bf16[2,32,128]{2,1,0:T(8,128)(2,1)} %slice_bitcast_fusion.own_ref), custom_call_target="tpu_custom_call" | custom-call | tf_op jit(solution)/shard_map/pallas_call | solution.py:168
  64.8 15.4 %all-to-all-done.1.recv_ref = bf16[32,256,128]{2,1,0:T(8,128)(2,1)S(1)} async-done(((bf16[32,256,128]{2,1,0:T(8,128)(2,1)}), bf16[32,256,128]{2,1,0:T(8,128)(2,1)S(1)}, u32[]{:S(2)}, u32[]{:S(2)}) %all-to-all-start.1) | async-done | bytes 2097184 | tf_op jit(solution)/shard_map/all_to_all | solution.py:157
  80.2 0.0 copy-start
  80.2 3.7 %all-to-all-start.3 = ((bf16[16,16,128]{2,1,0:T(8,128)(2,1)}), bf16[16,16,128]{2,1,0:T(8,128)(2,1)S(1)}, u32[]{:S(2)}, u32[]{:S(2)}) async-start(bf16[16,16,128]{2,1,0:T(8,128)(2,1)} %get-tuple-element.8), calls=%async_computation.3 | async-start | bytes 131072 | tf_op jit(solution)/shard_map/all_to_all | solution.py:182
  83.9 0.0 copy-done
  83.9 4.2 %shard_map.75 = bf16[32,64,128]{2,1,0:T(8,128)(2,1)} custom-call(bf16[8,128,512]{2,1,0:T(8,128)(2,1)} %get-tuple-element.7.panel_ref, bf16[32,256,128]{2,1,0:T(8,128)(2,1)} %copy-done), custom_call_target="tpu_custom_call" | custom-call | tf_op jit(solution)/shard_map/pallas_call | solution.py:185
  88.1 2.6 %all-to-all-done.3 = bf16[16,16,128]{2,1,0:T(8,128)(2,1)S(1)} async-done(((bf16[16,16,128]{2,1,0:T(8,128)(2,1)}), bf16[16,16,128]{2,1,0:T(8,128)(2,1)S(1)}, u32[]{:S(2)}, u32[]{:S(2)}) %all-to-all-start.3) | async-done | bytes 65568 | tf_op jit(solution)/shard_map/all_to_all | solution.py:182
  90.8 3.8 %all-to-all-start.2 = ((bf16[32,64,128]{2,1,0:T(8,128)(2,1)}), bf16[32,64,128]{2,1,0:T(8,128)(2,1)S(1)}, u32[]{:S(2)}, u32[]{:S(2)}) async-start(bf16[32,64,128]{2,1,0:T(8,128)(2,1)} %shard_map.75), calls=%async_computation.2 | async-start | bytes 1048576 | tf_op jit(solution)/shard_map/all_to_all | solution.py:196
  94.6 15.5 %all-to-all-done.2 = bf16[32,64,128]{2,1,0:T(8,128)(2,1)S(1)} async-done(((bf16[32,64,128]{2,1,0:T(8,128)(2,1)}), bf16[32,64,128]{2,1,0:T(8,128)(2,1)S(1)}, u32[]{:S(2)}, u32[]{:S(2)}) %all-to-all-start.2) | async-done | bytes 524320 | tf_op jit(solution)/shard_map/all_to_all | solution.py:196
  110.1 0.8 pad_maximum_fusion
  (1 shorter events, 0.0 us)
Async XLA Ops:
  0.0 12.9 %copy-start.1 = (bf16[129,2,32,128]{3,2,1,0:T(8,128)(2,1)S(1)}, bf16[129,2,32,128]{3,2,1,0:T(8,128)(2,1)}, u32[]{:S(2)}) copy-start(bf16[129,2,32,128]{3,2,1,0:T(8,128)(2,1)} %param.11) | copy-start | bytes 6340612
  5.6 21.8 %all-to-all-start = ((bf16[16,16,1024]{2,1,0:T(8,128)(2,1)}), bf16[16,16,1024]{2,1,0:T(8,128)(2,1)S(1)}, u32[]{:S(2)}, u32[]{:S(2)}) async-start(bf16[16,16,1024]{2,1,0:T(8,128)(2,1)} %shard_map.73), calls=%async_computation | async-start | bytes 1048576 | tf_op jit(solution)/shard_map/all_to_all | solution.py:166
  27.4 6.0 %copy-start.2 = (bf16[16,16,1024]{2,1,0:T(8,128)(2,1)}, bf16[16,16,1024]{2,1,0:T(8,128)(2,1)S(1)}, u32[]{:S(2)}) copy-start(bf16[16,16,1024]{2,1,0:T(8,128)(2,1)S(1)} %all-to-all-done.rows_ref) | copy-start | bytes 1572868
  27.4 52.8 %all-to-all-start.1 = ((bf16[32,256,128]{2,1,0:T(8,128)(2,1)}), bf16[32,256,128]{2,1,0:T(8,128)(2,1)S(1)}, u32[]{:S(2)}, u32[]{:S(2)}) async-start(bf16[32,256,128]{2,1,0:T(8,128)(2,1)} %bitcast.12), calls=%async_computation.1 | async-start | bytes 4194304 | tf_op jit(solution)/shard_map/all_to_all | solution.py:157
  80.2 3.7 %copy-start = (bf16[32,256,128]{2,1,0:T(8,128)(2,1)}, bf16[32,256,128]{2,1,0:T(8,128)(2,1)S(1)}, u32[]{:S(2)}) copy-start(bf16[32,256,128]{2,1,0:T(8,128)(2,1)S(1)} %all-to-all-done.1.recv_ref) | copy-start | bytes 6291460
  80.2 10.6 %all-to-all-start.3 = ((bf16[16,16,128]{2,1,0:T(8,128)(2,1)}), bf16[16,16,128]{2,1,0:T(8,128)(2,1)S(1)}, u32[]{:S(2)}, u32[]{:S(2)}) async-start(bf16[16,16,128]{2,1,0:T(8,128)(2,1)} %get-tuple-element.8), calls=%async_computation.3 | async-start | bytes 131072 | tf_op jit(solution)/shard_map/all_to_all | solution.py:182
  90.8 19.3 %all-to-all-start.2 = ((bf16[32,64,128]{2,1,0:T(8,128)(2,1)}), bf16[32,64,128]{2,1,0:T(8,128)(2,1)S(1)}, u32[]{:S(2)}, u32[]{:S(2)}) async-start(bf16[32,64,128]{2,1,0:T(8,128)(2,1)} %shard_map.75), calls=%async_computation.2 | async-start | bytes 1048576 | tf_op jit(solution)/shard_map/all_to_all | solution.py:196

commit v2 on v1

v2 whole, which is shorter than its diff:
```python
import functools
import math

import jax
import jax.numpy as jnp
import numpy as np
from jax import lax
from jax.experimental import pallas as pl
from jax.experimental.pallas import tpu as pltpu
from jax.sharding import PartitionSpec as P

SHOTS_PER_INDEX = 16
VMEM = pl.BlockSpec(memory_space=pltpu.VMEM)
LANES = 128
LIMIT = 16 * 1024 * 1024


def dft_tables(window, outer, across, inner, per, top):
    slots = 2 * per + 4
    n = np.arange(window, dtype=np.int64)
    table = np.zeros((outer, across, inner, slots, window), np.float64)
    for o in range(outer):
        for a in range(across):
            for i in range(inner):
                first = ((o * across + a) * inner + i) * per
                for j, f in enumerate(list(range(first, first + per)) + [top]):
                    angle = (n * f % window) * (2.0 * math.pi / window)
                    table[o, a, i, 2 * j] = np.cos(angle)
                    table[o, a, i, 2 * j + 1] = -np.sin(angle)
    table = (table / math.sqrt(window)).astype(np.float32)
    table = table.transpose(1, 0, 2, 3, 4).reshape(across, outer * inner * slots, window)
    high = table.astype(jnp.bfloat16)
    low = (table - high.astype(np.float32)).astype(jnp.bfloat16)
    return jnp.asarray(high), jnp.asarray(low), slots


def nt(a, b):
    return lax.dot_general(a, b, (((1,), (1,)), ((), ())), preferred_element_type=jnp.float32)


def spectra_kernel(slots, x_ref, high_ref, low_ref, block_ref, shot_ref, point_ref, out_ref):
    x = x_ref[...]
    mine = lax.axis_index("rcv") if high_ref.shape[0] > 1 else 0
    y = nt(high_ref[mine], x) + nt(low_ref[mine], x)
    shot = (block_ref[...] * SHOTS_PER_INDEX + shot_ref[...]).astype(jnp.float32)
    point = point_ref[...].astype(jnp.float32)
    for g in range(out_ref.shape[0]):
        pieces = []
        for j in range(x.shape[0] // LANES):
            lanes = slice(j * LANES, (j + 1) * LANES)
            pieces += [y[g * slots : (g + 1) * slots - 2, lanes], shot[:, lanes], point[:, lanes]]
        out_ref[g] = jnp.concatenate(pieces, axis=0).astype(jnp.bfloat16)


def bin_kernel(halves, shots, points, cols, rows_ref, own_ref, panel_ref, top_ref, acc_ref, top_acc_ref):
    sources = rows_ref.shape[0] // halves
    width = own_ref.shape[1]
    slots = cols + 4
    parts = rows_ref.shape[1] // slots
    own_shot, own_half = lax.axis_index("shot"), lax.axis_index("surf")

    def row(source, slot):
        return [rows_ref[source, j * slots + slot : j * slots + slot + 1, :] for j in range(parts)]

    def hits(source, count, slot, first):
        grid = lax.broadcasted_iota(jnp.int32, (count, LANES), 0).astype(jnp.float32)
        return [
            jnp.where(grid == ids.astype(jnp.float32) - first, 1.0, 0.0).astype(jnp.bfloat16)
            for ids in row(source, slot)
        ]

    def summed(into_ref, s, source, shot_hit, point_hit, chosen):
        for c, slot in enumerate(chosen):
            left = shot_hit if slot is None else [a * b for a, b in zip(shot_hit, row(source, slot))]
            got = nt(jnp.concatenate(left, axis=1), point_hit)
            into_ref[c] = jnp.where(s == 0, got, into_ref[c] + got)

    for half in range(halves):

        def step(s, carry):
            source = s * halves + half
            shot_hit = hits(source, shots, cols + 2, 0.0)
            point_hit = jnp.concatenate(hits(source, points, cols + 3, 0.0), axis=1)
            summed(acc_ref, s, source, shot_hit, point_hit, list(range(cols)) + [None])
            return carry

        lax.fori_loop(0, sources, step, 0)
        scale = 1.0 / jnp.maximum(acc_ref[cols], 1.0)
        for c in range(cols):
            panel_ref[c, :, half * points : (half + 1) * points] = (acc_ref[c] * scale).astype(jnp.bfloat16)

    def top_step(s, carry):
        source = s * halves + own_half
        shot_hit = hits(source, shots, cols + 2, 0.0)
        point_hit = jnp.concatenate(hits(source, width, cols + 3, (own_shot * width).astype(jnp.float32)), axis=1)
        summed(top_acc_ref, s, source, shot_hit, point_hit, [cols, cols + 1, None])
        return carry

    lax.fori_loop(0, sources, top_step, 0)
    scale = 1.0 / jnp.maximum(top_acc_ref[2], 1.0)
    real = (top_acc_ref[0] * scale).astype(jnp.bfloat16)
    imag = (top_acc_ref[1] * scale).astype(jnp.bfloat16)
    dot = functools.partial(jnp.dot, preferred_element_type=jnp.float32)
    own_real, own_imag = own_ref[0], own_ref[1]
    out_real = dot(real, own_real) - dot(imag, own_imag)
    out_imag = dot(real, own_imag) + dot(imag, own_real)
    targets = top_ref.shape[0]
    block = shots // targets
    for t in range(targets):
        rows = slice(t * block, (t + 1) * block)
        top_ref[t] = jnp.concatenate([out_real[rows], out_imag[rows]], axis=0).astype(jnp.bfloat16)


def product_kernel(n_shot, across, halves, width, panel_ref, recv_ref, top_ref, out_ref):
    per, shots = panel_ref.shape[0] // 2, panel_ref.shape[1]
    lanes = recv_ref.shape[2]
    block = shots // (n_shot * halves)
    for f in range(per):
        left = panel_ref[2 * f : 2 * f + 2].reshape(2 * shots, panel_ref.shape[2])
        sides = []
        for c in range(2):
            first = (2 * f + c) * width
            blocks = [
                jnp.concatenate(
                    [
                        recv_ref[(s * across + r) * halves + h, first : first + width, :]
                        for h in range(halves)
                        for s in range(n_shot)
                    ],
                    axis=0,
                )
                for r in range(across)
            ]
            right = blocks[0] if across == 1 else jnp.concatenate(blocks, axis=1)
            sides.append(jnp.dot(left, right, preferred_element_type=jnp.float32))
        real = sides[0][:shots] - sides[1][shots:]
        imag = sides[1][:shots] + sides[0][shots:]
        for s in range(n_shot):
            for h in range(halves):
                first = (s * halves + h) * block
                both = jnp.concatenate([real[first : first + block], imag[first : first + block]], axis=0)
                for r in range(across):
                    part = both[:, r * lanes : (r + 1) * lanes].astype(jnp.bfloat16)
                    out_ref[(s * across + r) * halves + h, 2 * f * block : 2 * (f + 1) * block, :] = part
    mine = lax.axis_index("rcv") if across > 1 else 0
    for s in range(n_shot):
        for h in range(halves):
            for r in range(across):
                part = top_ref[s * halves + h]
                part = jnp.where(mine == r, part, jnp.zeros_like(part))
                out_ref[(s * across + r) * halves + h, 2 * per * block :, :] = part


def gather_kernel(per, got_ref, out_ref):
    block = out_ref.shape[2]
    sources = got_ref.shape[0]
    total = got_ref[0, 2 * per * block :, :].astype(jnp.float32)
    for g in range(1, sources):
        total = total + got_ref[g, 2 * per * block :, :].astype(jnp.float32)
    for g in range(sources):
        out_ref[g * per : (g + 1) * per] = got_ref[g, : 2 * per * block, :].reshape((per,) + out_ref.shape[1:])
    out_ref[sources * per :] = total.astype(jnp.bfloat16).reshape((1,) + out_ref.shape[1:])


def call(kernel, out_shape, operands, scratch=(), limit=LIMIT):
    return pl.pallas_call(
        kernel,
        out_shape=out_shape,
        in_specs=[VMEM] * len(operands),
        out_specs=jax.tree.map(lambda _: VMEM, out_shape),
        scratch_shapes=list(scratch),
        compiler_params=pltpu.CompilerParams(vmem_limit_bytes=limit),
    )(*operands)


def local(traces, trace_block, trace_shot, trace_point, recv_panel):
    n_shot, n_rcv, halves = lax.axis_size("shot"), lax.axis_size("rcv"), lax.axis_size("surf")
    freqs, _, width, lanes = recv_panel.shape
    window, n_rows = traces.shape[2], traces.shape[1]
    shots, points = SHOTS_PER_INDEX * n_shot, width * n_shot
    assert max(shots, points) <= 256
    main = freqs - 1
    pairs = n_shot * halves
    across = n_rcv if main % (pairs * n_rcv) == 0 else 1
    axes = ("shot", "rcv", "surf") if across > 1 else ("shot", "surf")
    groups = pairs * across
    per = main // groups
    cols = 2 * per
    block = shots // pairs
    bf16 = functools.partial(jax.ShapeDtypeStruct, dtype=jnp.bfloat16)
    high, low, slots = dft_tables(window, n_shot, across, halves, per, main)

    recv = recv_panel[:main].reshape(groups, per * 2 * width, lanes)
    recv = lax.all_to_all(recv, axes, split_axis=0, concat_axis=0, tiled=True)

    message = call(
        functools.partial(spectra_kernel, slots),
        bf16((pairs, n_rows // LANES * slots, LANES)),
        (traces[0], high, low, trace_block.reshape(1, n_rows), trace_shot, trace_point),
        limit=56 * 1024 * 1024,
    )
    rows = lax.all_to_all(message, ("shot", "surf"), split_axis=0, concat_axis=0, tiled=True)

    panel, top = call(
        functools.partial(bin_kernel, halves, shots, points, cols),
        (bf16((cols, shots, halves * points)), bf16((pairs, 2 * block, lanes))),
        (rows, recv_panel[main]),
        (pltpu.VMEM((cols + 1, shots, points), jnp.float32), pltpu.VMEM((3, shots, width), jnp.float32)),
    )
    out = call(
        functools.partial(product_kernel, n_shot, across, halves, width),
        bf16((groups, (per + 1) * 2 * block, lanes)),
        (panel, recv, top),
    )
    out = lax.all_to_all(out, axes, split_axis=0, concat_axis=0, tiled=True)
    return call(functools.partial(gather_kernel, per), bf16((freqs, 2, block, lanes)), (out,))


def solution(mesh):
    in_specs = (
        P("surf", "shot", None),
        P("surf", "shot", None),
        P("surf", "shot"),
        P("surf", "shot"),
        P(None, None, ("shot", "surf"), "rcv"),
    )
    out_specs = P(None, None, ("shot", "surf"), "rcv")
    return jax.shard_map(local, mesh=mesh, in_specs=in_specs, out_specs=out_specs, check_vma=False)
```

time: 112 us -> 98.9 us (0.88)
  blocking collectives: 0 us -> 21.8 us
  waiting for transfers between devices: 46.2 us -> 26.5 us
  starting transfers between devices: 18.9 us -> 10.8 us
  Pallas kernels: 38.1 us -> 33.8 us
  other arithmetic: 2.9 us -> 0 us
    all_to_all x0 -> x1, blocking collectives: none -> 21.8 us  [local(): out = lax.all_to_all(out, axes, split_axis=0, concat_axis=0, tiled=True)]
    all_to_all x2 -> x0, waiting for transfers between devices: 18.2 us -> none  [the longest x1 15.5 us: local(): out = lax.all_to_all(out, axes, split_axis=0, concat_axis=0, tiled=True)]
    all_to_all x2 -> x0, starting transfers between devices: 7.46 us -> none  [the longest x1 3.79 us: local(): out = lax.all_to_all(out, axes, split_axis=0, concat_axis=0, tiled=True)]
    pallas_call x3 -> x4, Pallas kernels: 38.1 us -> 33.8 us  [call(): pl.pallas_call(kernel, out_shape=out_shape, in_specs=[VMEM] * len(operand...]
    all_to_all x1, waiting for transfers between devices: 12.7 us -> 8.83 us  [local(): lax.all_to_all(message, ('shot', 'surf'), split_axis=0, concat_axis=0, ti...]
    all_to_all x1, waiting for transfers between devices: 15.4 us -> 17.6 us  [local(): recv = lax.all_to_all(recv, axes, split_axis=0, concat_axis=0, tiled=True)]
    dynamic_slice x1 -> x0, local copies, waits for them, and re-layouts: 1.7 us -> none  [own_table(): lax.dynamic_index_in_dim(table, lax.axis_index('rcv') if spread else 0, 1...]
    slice x1, local copies, waits for them, and re-layouts: 1.76 us -> 3.37 us  [local(): recv = recv_panel[:main].reshape(groups, per * 2 * width, lanes)]
  transfers between devices with their start and end apart: 4 -> 2, of which waited for: 4 -> 2; matrix products, arithmetic and copies ran while one was open for 3% -> 4% of each run, Pallas kernels for 32% -> 30%
where the time goes in v2:
time: 98.9 us; the launch traced here: 98.5 us
  Pallas kernels  33.8 us (34%)
  waiting for transfers between devices  26.5 us (27%)
  blocking collectives  21.8 us (22%)
  starting transfers between devices  10.8 us (11%)
  local copies, waits for them, and re-layouts  5.55 us (6%)
    pallas_call x4, Pallas kernels, call(): pl.pallas_call(kernel, out_shape=out_shape, in_specs=[VMEM] * len(operand...  33.8 us
    all_to_all x1, blocking collectives, local(): out = lax.all_to_all(out, axes, split_axis=0, concat_axis=0, tiled=True)  21.8 us
    all_to_all x1, waiting for transfers between devices, local(): recv = lax.all_to_all(recv, axes, split_axis=0, concat_axis=0, tiled=True)  17.6 us
    all_to_all x1, waiting for transfers between devices, local(): lax.all_to_all(message, ('shot', 'surf'), split_axis=0, concat_axis=0, ti...  8.83 us
    all_to_all x1, starting transfers between devices, local(): lax.all_to_all(message, ('shot', 'surf'), split_axis=0, concat_axis=0, ti...  7.36 us
    all_to_all x1, starting transfers between devices, local(): recv = lax.all_to_all(recv, axes, split_axis=0, concat_axis=0, tiled=True)  3.46 us
    slice x1, local copies, waits for them, and re-layouts, local(): recv = recv_panel[:main].reshape(groups, per * 2 * width, lanes)  3.37 us
  transfers between devices with their start and end apart: 2, of which 2 were waited for; matrix products, arithmetic and copies ran while one was open for 4% of the time, Pallas kernels for 30%

profile of v2, /device:TPU:0, one launch (start us, length us, event | category | flops | bytes accessed | tf_op | source)
XLA Modules:
  0.0 98.5 jit_solution(15577697324756926276)
XLA Ops:
  0.0 2.5 %shard_map.73 = bf16[16,96,128]{2,1,0:T(8,128)(2,1)} custom-call(bf16[1024,256]{1,0:T(8,128)(2,1)} %bitcast.6, bf16[2,192,256]{2,1,0:T(8,128)(2,1)} %constant.4.clone.high_ref, bf16[2,192,256]{2,1,0:T(8,128)(2,1)} %constant.5.clone.low_ref, s32[1,1024]{1,0:T(1,128)} %bitcast.7, s32[1,1024]{1,0:T(1,128)} %shot_ref.1, s32[1,1024]{1,0:T(1,128)} %point_ref.1), custom_call_target="tpu_custom_call" | custom-call | tf_op jit(solution)/shard_map/pallas_call | solution.py:166
  2.5 7.4 %all-to-all-start = ((bf16[16,96,128]{2,1,0:T(8,128)(2,1)}), bf16[16,96,128]{2,1,0:T(8,128)(2,1)S(1)}, u32[]{:S(2)}, u32[]{:S(2)}) async-start(bf16[16,96,128]{2,1,0:T(8,128)(2,1)} %shard_map.73), calls=%async_computation | async-start | bytes 786432 | tf_op jit(solution)/shard_map/all_to_all | solution.py:202
  9.8 3.4 %slice.7 = bf16[128,2,32,128]{3,2,1,0:T(8,128)(2,1)} slice(bf16[129,2,32,128]{3,2,1,0:T(8,128)(2,1)} %param.11), slice={[0:128], [0:2], [0:32], [0:128]} | slice | bytes 4194304 | tf_op jit(solution)/shard_map/slice | solution.py:193
  13.2 8.8 %all-to-all-done.rows_ref = bf16[16,96,128]{2,1,0:T(8,128)(2,1)S(1)} async-done(((bf16[16,96,128]{2,1,0:T(8,128)(2,1)}), bf16[16,96,128]{2,1,0:T(8,128)(2,1)S(1)}, u32[]{:S(2)}, u32[]{:S(2)}) %all-to-all-start) | async-done | bytes 393248 | tf_op jit(solution)/shard_map/all_to_all | solution.py:202
  22.0 3.5 %all-to-all-start.1 = ((bf16[32,256,128]{2,1,0:T(8,128)(2,1)}), bf16[32,256,128]{2,1,0:T(8,128)(2,1)S(1)}, u32[]{:S(2)}, u32[]{:S(2)}) async-start(bf16[32,256,128]{2,1,0:T(8,128)(2,1)} %bitcast.5), calls=%async_computation.1 | async-start | bytes 4194304 | tf_op jit(solution)/shard_map/all_to_all | solution.py:194
  25.5 0.7 slice_bitcast_fusion.own_ref
  26.2 29.8 %shard_map.74 = (bf16[8,128,512]{2,1,0:T(8,128)(2,1)S(1)}, bf16[16,16,128]{2,1,0:T(8,128)(2,1)S(1)}) custom-call(bf16[16,96,128]{2,1,0:T(8,128)(2,1)S(1)} %all-to-all-done.rows_ref, bf16[2,32,128]{2,1,0:T(8,128)(2,1)S(1)} %slice_bitcast_fusion.own_ref), custom_call_target="tpu_custom_call" | custom-call | tf_op jit(solution)/shard_map/pallas_call | solution.py:166
  56.0 0.0 copy-start
  56.0 0.6 copy-done
  56.6 17.6 %all-to-all-done.1.recv_ref = bf16[32,256,128]{2,1,0:T(8,128)(2,1)S(1)} async-done(((bf16[32,256,128]{2,1,0:T(8,128)(2,1)}), bf16[32,256,128]{2,1,0:T(8,128)(2,1)S(1)}, u32[]{:S(2)}, u32[]{:S(2)}) %all-to-all-start.1) | async-done | bytes 2097184 | tf_op jit(solution)/shard_map/all_to_all | solution.py:194
  74.3 0.0 copy-start.1
  74.3 0.8 copy-done.1
  75.1 0.7 shard_map.75
  75.8 21.8 %all_to_all.15.got_ref = bf16[32,80,128]{2,1,0:T(8,128)(2,1)S(1)} all-to-all(bf16[32,80,128]{2,1,0:T(8,128)(2,1)S(1)} %shard_map.75), channel_id=1, replica_groups=mesh['shot'=8,'rcv'=2,'surf'=2] {'shot','rcv','surf'}, dimensions={0} | all-to-all | bytes 1310720 | tf_op jit(solution)/shard_map/all_to_all | solution.py:215
  97.6 0.9 shard_map.76
Async XLA Ops:
  2.5 19.6 %all-to-all-start = ((bf16[16,96,128]{2,1,0:T(8,128)(2,1)}), bf16[16,96,128]{2,1,0:T(8,128)(2,1)S(1)}, u32[]{:S(2)}, u32[]{:S(2)}) async-start(bf16[16,96,128]{2,1,0:T(8,128)(2,1)} %shard_map.73), calls=%async_computation | async-start | bytes 786432 | tf_op jit(solution)/shard_map/all_to_all | solution.py:202
  22.0 52.2 %all-to-all-start.1 = ((bf16[32,256,128]{2,1,0:T(8,128)(2,1)}), bf16[32,256,128]{2,1,0:T(8,128)(2,1)S(1)}, u32[]{:S(2)}, u32[]{:S(2)}) async-start(bf16[32,256,128]{2,1,0:T(8,128)(2,1)} %bitcast.5), calls=%async_computation.1 | async-start | bytes 4194304 | tf_op jit(solution)/shard_map/all_to_all | solution.py:194
  56.0 0.6 copy-start
  74.3 0.8 copy-start.1

commit v3 on v2

v3 whole, which is shorter than its diff:
```python
import functools
import math

import jax
import jax.numpy as jnp
import numpy as np
from jax import lax
from jax.experimental import pallas as pl
from jax.experimental.pallas import tpu as pltpu
from jax.sharding import Mesh
from jax.sharding import PartitionSpec as P

SHOTS_PER_INDEX = 16
VMEM = pl.BlockSpec(memory_space=pltpu.VMEM)
LANES = 128
LIMIT = 16 * 1024 * 1024


GROUPS = 2
STACK = 5
SHOT = ("group", "member")


def dft_tables(window, members, n_rcv, per, top):
    slots = -(-(2 * per + 4) // 16) * 16
    n = np.arange(window, dtype=np.int64)
    table = np.zeros((n_rcv, members, slots, window), np.float64)
    for r in range(n_rcv):
        for t in range(members):
            first = (t * n_rcv + r) * per
            for j, f in enumerate(list(range(first, first + per)) + [top]):
                angle = (n * f % window) * (2.0 * math.pi / window)
                table[r, t, 2 * j] = np.cos(angle)
                table[r, t, 2 * j + 1] = -np.sin(angle)
    table = (table / math.sqrt(window)).astype(np.float32)
    high = table.astype(jnp.bfloat16)
    low = (table - high.astype(np.float32)).astype(jnp.bfloat16)
    return jnp.asarray(high), jnp.asarray(low)


def nt(a, b):
    return lax.dot_general(a, b, (((1,), (1,)), ((), ())), preferred_element_type=jnp.float32)


def spectra_kernel(cols, x_ref, high_ref, low_ref, block_ref, shot_ref, point_ref, *out_refs):
    x = x_ref[...]
    mine, member = lax.axis_index("rcv"), lax.axis_index("member")
    high = jnp.concatenate([high_ref[mine, member ^ d] for d in range(len(out_refs))], axis=0)
    low = jnp.concatenate([low_ref[mine, member ^ d] for d in range(len(out_refs))], axis=0)
    y = nt(high, x) + nt(low, x)
    slots = high_ref.shape[2]
    shot = (block_ref[...] * SHOTS_PER_INDEX + shot_ref[...]).astype(jnp.float32)
    point = point_ref[...].astype(jnp.float32)
    for d, out_ref in enumerate(out_refs):
        pieces = []
        for j in range(x.shape[0] // LANES):
            lanes = slice(j * LANES, (j + 1) * LANES)
            pieces += [y[d * slots : d * slots + cols + 2, lanes], shot[:, lanes], point[:, lanes]]
        out_ref[...] = jnp.concatenate(pieces, axis=0).astype(jnp.bfloat16)


def bin_kernel(halves, shots, points, cols, n_sources, *refs):
    row_refs, own_ref = refs[:n_sources], refs[n_sources]
    panel_refs = refs[n_sources + 1 : n_sources + 1 + halves]
    top_ref, rows_ref, left_ref, acc_ref, pad_ref = refs[n_sources + 1 + halves :]
    width = own_ref.shape[1]
    slots = cols + 4
    parts = row_refs[0].shape[0] // slots
    group, member, own_half = (lax.axis_index(name) for name in ("group", "member", "surf"))
    for i, ref in enumerate(row_refs):
        rows_ref[i] = ref[...]
    acc_ref[...] = jnp.zeros_like(acc_ref)
    pad_ref[...] = jnp.zeros_like(pad_ref)
    pad_ref[:, pl.ds(pl.multiple_of(member * width, width), width), :] = own_ref[...]

    def hits(source, count, slot, first):
        grid = lax.broadcasted_iota(jnp.int32, (count, LANES), 0).astype(jnp.float32)
        ids = [rows_ref[source, j * slots + slot : j * slots + slot + 1, :] for j in range(parts)]
        return [jnp.where(grid == i.astype(jnp.float32) - first, 1.0, 0.0).astype(jnp.bfloat16) for i in ids]

    chosen = list(range(cols + 2)) + [None]

    def step(source, carry):
        shot_hit = hits(source, shots, cols + 2, 0.0)
        point_hit = jnp.concatenate(hits(source, points, cols + 3, (group * points).astype(jnp.float32)), axis=1)
        for first in range(0, len(chosen), STACK):
            stack = chosen[first : first + STACK]
            for i, slot in enumerate(stack):
                for j in range(parts):
                    left = shot_hit[j]
                    if slot is not None:
                        left = left * rows_ref[source, j * slots + slot : j * slots + slot + 1, :]
                    left_ref[i * shots : (i + 1) * shots, j * LANES : (j + 1) * LANES] = left
            got = nt(left_ref[: len(stack) * shots], point_hit)
            acc_ref[first : first + len(stack)] += got.reshape(len(stack), shots, points)
        return carry

    lax.fori_loop(0, n_sources, step, 0)
    scale = 1.0 / jnp.maximum(acc_ref[cols + 2], 1.0)
    each = cols // halves
    for k, ref in enumerate(panel_refs):
        for c in range(each):
            ref[c] = (acc_ref[(own_half ^ k) * each + c] * scale).astype(jnp.bfloat16)
    real = (acc_ref[cols] * scale).astype(jnp.bfloat16)
    imag = (acc_ref[cols + 1] * scale).astype(jnp.bfloat16)
    dot = functools.partial(jnp.dot, preferred_element_type=jnp.float32)
    out_real = dot(real, pad_ref[0]) - dot(imag, pad_ref[1])
    out_imag = dot(real, pad_ref[1]) + dot(imag, pad_ref[0])
    targets = top_ref.shape[0]
    block = shots // targets
    for t in range(targets):
        rows = slice(t * block, (t + 1) * block)
        top_ref[t] = jnp.concatenate([out_real[rows], out_imag[rows]], axis=0).astype(jnp.bfloat16)


def product_kernel(members, n_shot, n_rcv, halves, width, *refs):
    panel_refs, (recv_ref, top_ref, out_ref) = refs[:halves], refs[halves:]
    per, shots, points = panel_refs[0].shape[0] // 2, panel_refs[0].shape[1], panel_refs[0].shape[2]
    lanes = recv_ref.shape[2]
    block = shots // (n_shot * halves)
    own_half, mine = lax.axis_index("surf"), lax.axis_index("rcv")
    for f in range(per):
        left = [ref[2 * f : 2 * f + 2].reshape(2 * shots, points) for ref in panel_refs]
        left = jnp.concatenate(left, axis=1)
        sides = []
        for c in range(2):
            first = (2 * f + c) * width
            blocks = [
                jnp.concatenate(
                    [
                        recv_ref[(t * n_rcv + r) * halves + (own_half ^ k), first : first + width, :]
                        for k in range(halves)
                        for t in range(members)
                    ],
                    axis=0,
                )
                for r in range(n_rcv)
            ]
            right = blocks[0] if n_rcv == 1 else jnp.concatenate(blocks, axis=1)
            sides.append(jnp.dot(left, right, preferred_element_type=jnp.float32))
        real = sides[0][:shots] - sides[1][shots:]
        imag = sides[1][:shots] + sides[0][shots:]
        for s in range(n_shot):
            for h in range(halves):
                first = (s * halves + h) * block
                both = jnp.concatenate([real[first : first + block], imag[first : first + block]], axis=0)
                for r in range(n_rcv):
                    part = both[:, r * lanes : (r + 1) * lanes].astype(jnp.bfloat16)
                    out_ref[(s * n_rcv + r) * halves + h, 2 * f * block : 2 * (f + 1) * block, :] = part
    for s in range(n_shot):
        for h in range(halves):
            for r in range(n_rcv):
                part = top_ref[s * halves + h]
                part = jnp.where(mine == r, part, jnp.zeros_like(part))
                out_ref[(s * n_rcv + r) * halves + h, 2 * per * block :, :] = part


def gather_kernel(per, groups, got_ref, out_ref):
    block = out_ref.shape[2]
    each = got_ref.shape[0] // groups
    rows = 2 * per * block
    total = jnp.zeros((2 * block, got_ref.shape[2]), jnp.float32)
    for w in range(each):
        value = jnp.zeros((rows, got_ref.shape[2]), jnp.float32)
        for g in range(groups):
            value = value + got_ref[g * each + w, :rows, :].astype(jnp.float32)
            total = total + got_ref[g * each + w, rows:, :].astype(jnp.float32)
        out_ref[w * per : (w + 1) * per] = value.reshape((per,) + out_ref.shape[1:]).astype(jnp.bfloat16)
    out_ref[each * per :] = total.reshape((1,) + out_ref.shape[1:]).astype(jnp.bfloat16)


def call(kernel, out_shape, operands, scratch=(), limit=LIMIT):
    return pl.pallas_call(
        kernel,
        out_shape=out_shape,
        in_specs=[VMEM] * len(operands),
        out_specs=jax.tree.map(lambda _: VMEM, out_shape),
        scratch_shapes=list(scratch),
        compiler_params=pltpu.CompilerParams(vmem_limit_bytes=limit),
    )(*operands)


def local(traces, trace_block, trace_shot, trace_point, recv_panel):
    groups, members = lax.axis_size("group"), lax.axis_size("member")
    n_shot, n_rcv, halves = groups * members, lax.axis_size("rcv"), lax.axis_size("surf")
    freqs, _, width, lanes = recv_panel.shape
    window, n_rows = traces.shape[2], traces.shape[1]
    shots, points = SHOTS_PER_INDEX * n_shot, width * members
    assert max(shots, points * groups) <= 256
    main = freqs - 1
    owners = members * n_rcv * halves
    per = main // owners
    assert per * owners == main
    cols = 2 * per * halves
    block = shots // (n_shot * halves)
    bf16 = functools.partial(jax.ShapeDtypeStruct, dtype=jnp.bfloat16)
    high, low = dft_tables(window, members, n_rcv, per * halves, main)

    messages = call(
        functools.partial(spectra_kernel, cols),
        (bf16((n_rows // LANES * (cols + 4), LANES)),) * members,
        (traces[0], high, low, trace_block.reshape(1, n_rows), trace_shot, trace_point),
        limit=56 * 1024 * 1024,
    )
    rows = [messages[0]]
    for d in range(1, n_shot):
        rows.append(lax.ppermute(messages[d % members], SHOT, [(s, s ^ d) for s in range(n_shot)]))

    recv = recv_panel[:main].reshape(owners, per * 2 * width, lanes)
    recv, *rows = lax.optimization_barrier((recv, *rows))
    recv = lax.all_to_all(recv, ("member", "rcv", "surf"), split_axis=0, concat_axis=0, tiled=True)

    panel = bf16((2 * per, shots, points))
    *panels, top = call(
        functools.partial(bin_kernel, halves, shots, points, cols, n_shot),
        (panel,) * halves + (bf16((n_shot * halves, 2 * block, lanes)),),
        (*rows, recv_panel[main]),
        (
            pltpu.VMEM((n_shot,) + rows[0].shape, jnp.bfloat16),
            pltpu.VMEM((STACK * shots, n_rows), jnp.bfloat16),
            pltpu.VMEM((cols + 3, shots, points), jnp.float32),
            pltpu.VMEM((2, points, lanes), jnp.bfloat16),
        ),
    )
    for k in range(1, halves):
        panels[k] = lax.ppermute(panels[k], "surf", [(h, h ^ k) for h in range(halves)])
    out = call(
        functools.partial(product_kernel, members, n_shot, n_rcv, halves, width),
        bf16((n_shot * n_rcv * halves, (per + 1) * 2 * block, lanes)),
        (*panels, recv, top),
    )
    out = lax.all_to_all(out, SHOT + ("rcv", "surf"), split_axis=0, concat_axis=0, tiled=True)
    return call(functools.partial(gather_kernel, per, groups), bf16((freqs, 2, block, lanes)), (out,))


def solution(mesh):
    n_shot, n_rcv, halves = (mesh.shape[name] for name in ("shot", "rcv", "surf"))
    devices = mesh.devices.reshape(GROUPS, n_shot // GROUPS, n_rcv, halves)
    mesh = Mesh(devices, SHOT + ("rcv", "surf"))
    in_specs = (
        P("surf", SHOT, None),
        P("surf", SHOT, None),
        P("surf", SHOT),
        P("surf", SHOT),
        P(None, None, SHOT + ("surf",), "rcv"),
    )
    out_specs = P(None, None, SHOT + ("surf",), "rcv")
    return jax.shard_map(local, mesh=mesh, in_specs=in_specs, out_specs=out_specs, check_vma=False)
```

time: 98.9 us -> 93 us (0.940)
  waiting for transfers between devices: 26.5 us -> 6.95 us
  blocking collectives: 21.8 us -> 34.5 us
  starting transfers between devices: 10.8 us -> 19.3 us
  Pallas kernels: 33.8 us -> 27.9 us
  local copies, waits for them, and re-layouts: 5.55 us -> 4.07 us
    all_to_all x2 -> x1, waiting for transfers between devices: 26.5 us -> 3.22 us  [local(): lax.all_to_all(recv, ('member', 'rcv', 'surf'), split_axis=0, concat_axis...]
    ppermute x0 -> x8, starting transfers between devices: none -> 15.5 us  [the longest x7 15.1 us: local(): lax.ppermute(messages[d % members], SHOT, [(s, s ^ d) for s in range(n_sh...]
    all_to_all x1, blocking collectives: 21.8 us -> 34.5 us  [local(): lax.all_to_all(out, SHOT + ('rcv', 'surf'), split_axis=0, concat_axis=0,...]
    all_to_all x2 -> x1, starting transfers between devices: 10.8 us -> 3.85 us  [local(): lax.all_to_all(recv, ('member', 'rcv', 'surf'), split_axis=0, concat_axis...]
    pallas_call x4, Pallas kernels: 33.8 us -> 27.9 us  [call(): pl.pallas_call(kernel, out_shape=out_shape, in_specs=[VMEM] * len(operand...]
    ppermute x0 -> x8, waiting for transfers between devices: none -> 3.73 us  [the longest x7 2.11 us: local(): lax.ppermute(messages[d % members], SHOT, [(s, s ^ d) for s in range(n_sh...]
    unnamed x4 -> x2, local copies, waits for them, and re-layouts: 1.46 us -> 0.01 us
  transfers between devices with their start and end apart: 2 -> 9, of which waited for: 2 -> 3; matrix products, arithmetic and copies ran while one was open for 4% -> 4% of each run, Pallas kernels for 30% -> 26%
where the time goes in v3:
time: 93 us; the launch traced here: 92.7 us
  blocking collectives  34.5 us (37%)
  Pallas kernels  27.9 us (30%)
  starting transfers between devices  19.3 us (21%)
  waiting for transfers between devices  6.95 us (7%)
  local copies, waits for them, and re-layouts  4.07 us (4%)
    all_to_all x1, blocking collectives, local(): lax.all_to_all(out, SHOT + ('rcv', 'surf'), split_axis=0, concat_axis=0,...  34.5 us
    pallas_call x4, Pallas kernels, call(): pl.pallas_call(kernel, out_shape=out_shape, in_specs=[VMEM] * len(operand...  27.9 us
    ppermute x7, starting transfers between devices, local(): lax.ppermute(messages[d % members], SHOT, [(s, s ^ d) for s in range(n_sh...  15.1 us
    all_to_all x1, starting transfers between devices, local(): lax.all_to_all(recv, ('member', 'rcv', 'surf'), split_axis=0, concat_axis...  3.85 us
    slice x1, local copies, waits for them, and re-layouts, local(): recv = recv_panel[:main].reshape(owners, per * 2 * width, lanes)  3.34 us
    all_to_all x1, waiting for transfers between devices, local(): lax.all_to_all(recv, ('member', 'rcv', 'surf'), split_axis=0, concat_axis...  3.22 us
    ppermute x7, waiting for transfers between devices, local(): lax.ppermute(messages[d % members], SHOT, [(s, s ^ d) for s in range(n_sh...  2.11 us
  transfers between devices with their start and end apart: 9, of which 3 were waited for; matrix products, arithmetic and copies ran while one was open for 4% of the time, Pallas kernels for 26%

profile of v3, /device:TPU:0, one launch (start us, length us, event | category | flops | bytes accessed | tf_op | source)
XLA Modules:
  0.0 92.7 jit_solution(14023579077496116327)
XLA Ops:
  0.0 2.3 %shard_map.73 = (bf16[288,128]{1,0:T(8,128)(2,1)}, bf16[288,128]{1,0:T(8,128)(2,1)}, bf16[288,128]{1,0:T(8,128)(2,1)}, bf16[288,128]{1,0:T(8,128)(2,1)}) custom-call(bf16[1024,256]{1,0:T(8,128)(2,1)} %bitcast.6, bf16[2,4,48,256]{3,2,1,0:T(8,128)(2,1)} %constant.4.clone.high_ref, bf16[2,4,48,256]{3,2,1,0:T(8,128)(2,1)} %constant.5.clone.low_ref, ...), custom_call_target="tpu_custom_call" | custom-call | tf_op jit(solution)/shard_map/pallas_call | solution.py:173
  2.4 4.0 %collective-permute-start.3 = (bf16[288,128]{1,0:T(8,128)(2,1)}, bf16[288,128]{1,0:T(8,128)(2,1)S(1)}, u32[]{:S(2)}, u32[]{:S(2)}) collective-permute-start(bf16[288,128]{1,0:T(8,128)(2,1)} %get-tuple-element.25.refs_0_), channel_id=1, source_target_pairs={{0,16},{4,20},{8,24},{12,28},{16,0},{20,4},{24,8},{28,12},{1,17},{... | collective-permute-start | bytes 221192 | tf_op jit(solution)/shard_map/ppermute | solution.py:207
  6.4 1.3 %collective-permute-start.4 = (bf16[288,128]{1,0:T(8,128)(2,1)}, bf16[288,128]{1,0:T(8,128)(2,1)S(1)}, u32[]{:S(2)}, u32[]{:S(2)}) collective-permute-start(bf16[288,128]{1,0:T(8,128)(2,1)} %get-tuple-element.22), channel_id=1, source_target_pairs={{0,20},{4,16},{8,28},{12,24},{16,4},{20,0},{24,12},{28,8},{1,21},{... | collective-permute-start | bytes 221192 | tf_op jit(solution)/shard_map/ppermute | solution.py:207
  7.7 0.2 collective-permute-start
  7.9 3.9 %collective-permute-start.5 = (bf16[288,128]{1,0:T(8,128)(2,1)}, bf16[288,128]{1,0:T(8,128)(2,1)S(1)}, u32[]{:S(2)}, u32[]{:S(2)}) collective-permute-start(bf16[288,128]{1,0:T(8,128)(2,1)} %get-tuple-element.23), channel_id=1, source_target_pairs={{0,24},{4,28},{8,16},{12,20},{16,8},{20,12},{24,0},{28,4},{1,25},{... | collective-permute-start | bytes 221192 | tf_op jit(solution)/shard_map/ppermute | solution.py:207
  11.8 0.0 collective-permute-start.1
  11.8 0.0 collective-permute-done.3.refs_4_
  11.8 5.7 %collective-permute-start.6 = (bf16[288,128]{1,0:T(8,128)(2,1)}, bf16[288,128]{1,0:T(8,128)(2,1)S(1)}, u32[]{:S(2)}, u32[]{:S(2)}) collective-permute-start(bf16[288,128]{1,0:T(8,128)(2,1)} %get-tuple-element.24), channel_id=1, source_target_pairs={{0,28},{4,24},{8,20},{12,16},{16,12},{20,8},{24,4},{28,0},{1,29},{... | collective-permute-start | bytes 221192 | tf_op jit(solution)/shard_map/ppermute | solution.py:207
  17.5 0.0 collective-permute-done.4.refs_5_
  17.5 0.0 collective-permute-start.2
  17.5 3.3 %slice.6 = bf16[128,2,32,128]{3,2,1,0:T(8,128)(2,1)} slice(bf16[129,2,32,128]{3,2,1,0:T(8,128)(2,1)} %param.11), slice={[0:128], [0:2], [0:32], [0:128]} | slice | bytes 4194304 | tf_op jit(solution)/shard_map/slice | solution.py:209
  20.8 0.0 collective-permute-done.refs_1_
  20.8 0.0 collective-permute-done.5.refs_6_
  20.8 0.0 collective-permute-done.1.refs_2_
  20.8 0.0 collective-permute-done.6.refs_7_
  20.8 2.1 %collective-permute-done.2.refs_3_ = bf16[288,128]{1,0:T(8,128)(2,1)S(1)} collective-permute-done((bf16[288,128]{1,0:T(8,128)(2,1)}, bf16[288,128]{1,0:T(8,128)(2,1)S(1)}, u32[]{:S(2)}, u32[]{:S(2)}) %collective-permute-start.2) | collective-permute-done | bytes 73760 | tf_op jit(solution)/shard_map/ppermute | solution.py:207
  22.9 0.0 copy-start
  22.9 3.8 %all-to-all-start = ((bf16[16,512,128]{2,1,0:T(8,128)(2,1)}), bf16[16,512,128]{2,1,0:T(8,128)(2,1)S(1)}, u32[]{:S(2)}, u32[]{:S(2)}) async-start(bf16[16,512,128]{2,1,0:T(8,128)(2,1)} %bitcast.5), calls=%async_computation | async-start | bytes 4194304 | tf_op jit(solution)/shard_map/all_to_all | solution.py:211
  26.8 0.7 slice_bitcast_fusion.refs_8_
  27.5 0.0 copy-done
  27.5 23.8 %shard_map.74 = (bf16[16,128,128]{2,1,0:T(8,128)(2,1)S(1)}, bf16[16,128,128]{2,1,0:T(8,128)(2,1)S(1)}, bf16[16,16,128]{2,1,0:T(8,128)(2,1)S(1)}) custom-call(bf16[288,128]{1,0:T(8,128)(2,1)S(1)} %copy-done, bf16[288,128]{1,0:T(8,128)(2,1)S(1)} %collective-permute-done.refs_1_, bf16[288,128]{1,0:T(8,128)(2,1)S(1)} %collective-permute-done.1.refs_2_, ...), custom_call_target="tpu_custom_call" | custom-call | tf_op jit(solution)/shard_map/pallas_call | solution.py:173
  51.4 0.4 collective-permute-start.7
  51.7 1.6 %collective-permute-done.7.refs_1_ = bf16[16,128,128]{2,1,0:T(8,128)(2,1)S(1)} collective-permute-done((bf16[16,128,128]{2,1,0:T(8,128)(2,1)S(1)}, bf16[16,128,128]{2,1,0:T(8,128)(2,1)S(1)}, u32[]{:S(2)}, u32[]{:S(2)}) %collective-permute-start.7) | collective-permute-done | bytes 524320 | tf_op jit(solution)/shard_map/ppermute | solution.py:226
  53.3 3.2 %all-to-all-done.refs_2_ = bf16[16,512,128]{2,1,0:T(8,128)(2,1)S(1)} async-done(((bf16[16,512,128]{2,1,0:T(8,128)(2,1)}), bf16[16,512,128]{2,1,0:T(8,128)(2,1)S(1)}, u32[]{:S(2)}, u32[]{:S(2)}) %all-to-all-start) | async-done | bytes 2097184 | tf_op jit(solution)/shard_map/all_to_all | solution.py:211
  56.6 0.7 shard_map.75
  57.3 34.5 %all_to_all.10.got_ref = bf16[32,144,128]{2,1,0:T(8,128)(2,1)S(1)} all-to-all(bf16[32,144,128]{2,1,0:T(8,128)(2,1)S(1)} %shard_map.75), channel_id=1, replica_groups=mesh['group'=2,'member'=4,'rcv'=2,'surf'=2] {'group','member','rcv','surf'}, dimensions={0} | all-to-all | bytes 2359296 | tf_op jit(solution)/shard_map/all_to_all | solution.py:232
  91.8 0.9 %shard_map.76 = bf16[129,2,8,128]{3,2,1,0:T(8,128)(2,1)} custom-call(bf16[32,144,128]{2,1,0:T(8,128)(2,1)S(1)} %all_to_all.10.got_ref), custom_call_target="tpu_custom_call" | custom-call | tf_op jit(solution)/shard_map/pallas_call | solution.py:173
Async XLA Ops:
  2.4 9.4 %collective-permute-start.3 = (bf16[288,128]{1,0:T(8,128)(2,1)}, bf16[288,128]{1,0:T(8,128)(2,1)S(1)}, u32[]{:S(2)}, u32[]{:S(2)}) collective-permute-start(bf16[288,128]{1,0:T(8,128)(2,1)} %get-tuple-element.25.refs_0_), channel_id=1, source_target_pairs={{0,16},{4,20},{8,24},{12,28},{16,0},{20,4},{24,8},{28,12},{1,17},{... | collective-permute-start | bytes 221192 | tf_op jit(solution)/shard_map/ppermute | solution.py:207
  6.4 11.1 %collective-permute-start.4 = (bf16[288,128]{1,0:T(8,128)(2,1)}, bf16[288,128]{1,0:T(8,128)(2,1)S(1)}, u32[]{:S(2)}, u32[]{:S(2)}) collective-permute-start(bf16[288,128]{1,0:T(8,128)(2,1)} %get-tuple-element.22), channel_id=1, source_target_pairs={{0,20},{4,16},{8,28},{12,24},{16,4},{20,0},{24,12},{28,8},{1,21},{... | collective-permute-start | bytes 221192 | tf_op jit(solution)/shard_map/ppermute | solution.py:207
  7.7 13.2 %collective-permute-start = (bf16[288,128]{1,0:T(8,128)(2,1)}, bf16[288,128]{1,0:T(8,128)(2,1)S(1)}, u32[]{:S(2)}, u32[]{:S(2)}) collective-permute-start(bf16[288,128]{1,0:T(8,128)(2,1)} %get-tuple-element.22), channel_id=1, source_target_pairs={{0,4},{4,0},{8,12},{12,8},{16,20},{20,16},{24,28},{28,24},{1,5},{5... | collective-permute-start | bytes 221192 | tf_op jit(solution)/shard_map/ppermute | solution.py:207
  7.9 12.9 %collective-permute-start.5 = (bf16[288,128]{1,0:T(8,128)(2,1)}, bf16[288,128]{1,0:T(8,128)(2,1)S(1)}, u32[]{:S(2)}, u32[]{:S(2)}) collective-permute-start(bf16[288,128]{1,0:T(8,128)(2,1)} %get-tuple-element.23), channel_id=1, source_target_pairs={{0,24},{4,28},{8,16},{12,20},{16,8},{20,12},{24,0},{28,4},{1,25},{... | collective-permute-start | bytes 221192 | tf_op jit(solution)/shard_map/ppermute | solution.py:207
  11.8 9.0 %collective-permute-start.1 = (bf16[288,128]{1,0:T(8,128)(2,1)}, bf16[288,128]{1,0:T(8,128)(2,1)S(1)}, u32[]{:S(2)}, u32[]{:S(2)}) collective-permute-start(bf16[288,128]{1,0:T(8,128)(2,1)} %get-tuple-element.23), channel_id=1, source_target_pairs={{0,8},{4,12},{8,0},{12,4},{16,24},{20,28},{24,16},{28,20},{1,9},{5... | collective-permute-start | bytes 221192 | tf_op jit(solution)/shard_map/ppermute | solution.py:207
  11.8 9.0 %collective-permute-start.6 = (bf16[288,128]{1,0:T(8,128)(2,1)}, bf16[288,128]{1,0:T(8,128)(2,1)S(1)}, u32[]{:S(2)}, u32[]{:S(2)}) collective-permute-start(bf16[288,128]{1,0:T(8,128)(2,1)} %get-tuple-element.24), channel_id=1, source_target_pairs={{0,28},{4,24},{8,20},{12,16},{16,12},{20,8},{24,4},{28,0},{1,29},{... | collective-permute-start | bytes 221192 | tf_op jit(solution)/shard_map/ppermute | solution.py:207
  17.5 5.5 %collective-permute-start.2 = (bf16[288,128]{1,0:T(8,128)(2,1)}, bf16[288,128]{1,0:T(8,128)(2,1)S(1)}, u32[]{:S(2)}, u32[]{:S(2)}) collective-permute-start(bf16[288,128]{1,0:T(8,128)(2,1)} %get-tuple-element.24), channel_id=1, source_target_pairs={{0,12},{4,8},{8,4},{12,0},{16,28},{20,24},{24,20},{28,16},{1,13},{... | collective-permute-start | bytes 221192 | tf_op jit(solution)/shard_map/ppermute | solution.py:207
  22.9 4.6 %copy-start = (bf16[288,128]{1,0:T(8,128)(2,1)S(1)}, bf16[288,128]{1,0:T(8,128)(2,1)}, u32[]{:S(2)}) copy-start(bf16[288,128]{1,0:T(8,128)(2,1)} %get-tuple-element.25.refs_0_) | copy-start | bytes 221188
  22.9 33.6 %all-to-all-start = ((bf16[16,512,128]{2,1,0:T(8,128)(2,1)}), bf16[16,512,128]{2,1,0:T(8,128)(2,1)S(1)}, u32[]{:S(2)}, u32[]{:S(2)}) async-start(bf16[16,512,128]{2,1,0:T(8,128)(2,1)} %bitcast.5), calls=%async_computation | async-start | bytes 4194304 | tf_op jit(solution)/shard_map/all_to_all | solution.py:211
  51.4 2.0 %collective-permute-start.7 = (bf16[16,128,128]{2,1,0:T(8,128)(2,1)S(1)}, bf16[16,128,128]{2,1,0:T(8,128)(2,1)S(1)}, u32[]{:S(2)}, u32[]{:S(2)}) collective-permute-start(bf16[16,128,128]{2,1,0:T(8,128)(2,1)S(1)} %get-tuple-element.34), channel_id=1, source_target_pairs={{0,1},{1,0},{2,3},{3,2},{4,5},{5,4},{6,7},{7,6},{8,9},{9,8},{10,11... | collective-permute-start | bytes 1572872 | tf_op jit(solution)/shard_map/ppermute | solution.py:226

commit v4 on v3

--- a/solution.py
+++ b/solution.py
@@ -17,6 +17,7 @@
 
 
 GROUPS = 2
+NEAR, FAR = 12, 12
 STACK = 5
 SHOT = ("group", "member")
 
@@ -45,10 +46,9 @@
 def spectra_kernel(cols, x_ref, high_ref, low_ref, block_ref, shot_ref, point_ref, *out_refs):
     x = x_ref[...]
     mine, member = lax.axis_index("rcv"), lax.axis_index("member")
-    high = jnp.concatenate([high_ref[mine, member ^ d] for d in range(len(out_refs))], axis=0)
-    low = jnp.concatenate([low_ref[mine, member ^ d] for d in range(len(out_refs))], axis=0)
-    y = nt(high, x) + nt(low, x)
     slots = high_ref.shape[2]
+    y = nt(jnp.concatenate([ref[mine, member ^ d] for ref in (high_ref, low_ref) for d in range(len(out_refs))], axis=0), x)
+    y = y[: slots * len(out_refs)] + y[slots * len(out_refs) :]
     shot = (block_ref[...] * SHOTS_PER_INDEX + shot_ref[...]).astype(jnp.float32)
     point = point_ref[...].astype(jnp.float32)
     for d, out_ref in enumerate(out_refs):
@@ -59,19 +59,11 @@
         out_ref[...] = jnp.concatenate(pieces, axis=0).astype(jnp.bfloat16)
 
 
-def bin_kernel(halves, shots, points, cols, n_sources, *refs):
-    row_refs, own_ref = refs[:n_sources], refs[n_sources]
-    panel_refs = refs[n_sources + 1 : n_sources + 1 + halves]
-    top_ref, rows_ref, left_ref, acc_ref, pad_ref = refs[n_sources + 1 + halves :]
-    width = own_ref.shape[1]
+def add_rows(cols, rows_ref, left_ref, acc_ref):
+    _, shots, points = acc_ref.shape
     slots = cols + 4
-    parts = row_refs[0].shape[0] // slots
-    group, member, own_half = (lax.axis_index(name) for name in ("group", "member", "surf"))
-    for i, ref in enumerate(row_refs):
-        rows_ref[i] = ref[...]
-    acc_ref[...] = jnp.zeros_like(acc_ref)
-    pad_ref[...] = jnp.zeros_like(pad_ref)
-    pad_ref[:, pl.ds(pl.multiple_of(member * width, width), width), :] = own_ref[...]
+    parts = rows_ref.shape[1] // slots
+    group = lax.axis_index("group")
 
     def hits(source, count, slot, first):
         grid = lax.broadcasted_iota(jnp.int32, (count, LANES), 0).astype(jnp.float32)
@@ -95,7 +87,22 @@
             acc_ref[first : first + len(stack)] += got.reshape(len(stack), shots, points)
         return carry
 
-    lax.fori_loop(0, n_sources, step, 0)
+    lax.fori_loop(0, rows_ref.shape[0], step, 0)
+
+
+def near_kernel(cols, rows_ref, acc_ref, left_ref):
+    acc_ref[...] = jnp.zeros_like(acc_ref)
+    add_rows(cols, rows_ref, left_ref, acc_ref)
+
+
+def far_kernel(cols, halves, rows_ref, near_ref, own_ref, *refs):
+    panel_refs, (left_ref, acc_ref, pad_ref) = refs[:halves], refs[halves:]
+    width = own_ref.shape[1]
+    member, own_half = lax.axis_index("member"), lax.axis_index("surf")
+    pad_ref[...] = jnp.zeros_like(pad_ref)
+    pad_ref[:, pl.ds(pl.multiple_of(member * width, width), width), :] = own_ref[...]
+    acc_ref[...] = near_ref[...]
+    add_rows(cols, rows_ref, left_ref, acc_ref)
     scale = 1.0 / jnp.maximum(acc_ref[cols + 2], 1.0)
     each = cols // halves
     for k, ref in enumerate(panel_refs):
@@ -106,16 +113,14 @@
     dot = functools.partial(jnp.dot, preferred_element_type=jnp.float32)
     out_real = dot(real, pad_ref[0]) - dot(imag, pad_ref[1])
     out_imag = dot(real, pad_ref[1]) + dot(imag, pad_ref[0])
-    targets = top_ref.shape[0]
-    block = shots // targets
-    for t in range(targets):
-        rows = slice(t * block, (t + 1) * block)
-        top_ref[t] = jnp.concatenate([out_real[rows], out_imag[rows]], axis=0).astype(jnp.bfloat16)
+    for ref in panel_refs:
+        ref[each] = out_real.astype(jnp.bfloat16)
+        ref[each + 1] = out_imag.astype(jnp.bfloat16)
 
 
 def product_kernel(members, n_shot, n_rcv, halves, width, *refs):
-    panel_refs, (recv_ref, top_ref, out_ref) = refs[:halves], refs[halves:]
-    per, shots, points = panel_refs[0].shape[0] // 2, panel_refs[0].shape[1], panel_refs[0].shape[2]
+    panel_refs, (recv_ref, out_ref) = refs[:halves], refs[halves:]
+    per, shots, points = panel_refs[0].shape[0] // 2 - 1, panel_refs[0].shape[1], panel_refs[0].shape[2]
     lanes = recv_ref.shape[2]
     block = shots // (n_shot * halves)
     own_half, mine = lax.axis_index("surf"), lax.axis_index("rcv")
@@ -147,29 +152,33 @@
                 for r in range(n_rcv):
                     part = both[:, r * lanes : (r + 1) * lanes].astype(jnp.bfloat16)
                     out_ref[(s * n_rcv + r) * halves + h, 2 * f * block : 2 * (f + 1) * block, :] = part
-    for s in range(n_shot):
-        for h in range(halves):
-            for r in range(n_rcv):
-                part = top_ref[s * halves + h]
-                part = jnp.where(mine == r, part, jnp.zeros_like(part))
-                out_ref[(s * n_rcv + r) * halves + h, 2 * per * block :, :] = part
-
-
-def gather_kernel(per, groups, got_ref, out_ref):
+    top = panel_refs[0][2 * per + own_half].astype(jnp.float32)
+    for ref in panel_refs[1:]:
+        top = top + ref[2 * per + own_half].astype(jnp.float32)
+    for r in range(n_rcv):
+        part = jnp.where(mine == r, top, jnp.zeros_like(top)).astype(jnp.bfloat16)
+        for s in range(n_shot):
+            for h in range(halves):
+                first = (s * halves + h) * block
+                out_ref[(s * n_rcv + r) * halves + h, 2 * per * block :, :] = part[first : first + block]
+
+
+def gather_kernel(per, groups, halves, got_ref, out_ref):
     block = out_ref.shape[2]
     each = got_ref.shape[0] // groups
     rows = 2 * per * block
-    total = jnp.zeros((2 * block, got_ref.shape[2]), jnp.float32)
+    tops = [jnp.zeros((block, got_ref.shape[2]), jnp.float32) for _ in range(halves)]
     for w in range(each):
         value = jnp.zeros((rows, got_ref.shape[2]), jnp.float32)
         for g in range(groups):
             value = value + got_ref[g * each + w, :rows, :].astype(jnp.float32)
-            total = total + got_ref[g * each + w, rows:, :].astype(jnp.float32)
+            tops[w % halves] = tops[w % halves] + got_ref[g * each + w, rows:, :].astype(jnp.float32)
         out_ref[w * per : (w + 1) * per] = value.reshape((per,) + out_ref.shape[1:]).astype(jnp.bfloat16)
-    out_ref[each * per :] = total.reshape((1,) + out_ref.shape[1:]).astype(jnp.bfloat16)
-
-
-def call(kernel, out_shape, operands, scratch=(), limit=LIMIT):
+    for c in range(halves):
+        out_ref[each * per, c] = tops[c].astype(jnp.bfloat16)
+
+
+def call(kernel, out_shape, operands, scratch=(), limit=LIMIT, flops=None):
     return pl.pallas_call(
         kernel,
         out_shape=out_shape,
@@ -177,6 +186,7 @@
         out_specs=jax.tree.map(lambda _: VMEM, out_shape),
         scratch_shapes=list(scratch),
         compiler_params=pltpu.CompilerParams(vmem_limit_bytes=limit),
+        cost_estimate=flops and pl.CostEstimate(flops=flops, transcendentals=0, bytes_accessed=0),
     )(*operands)
 
 
@@ -190,47 +200,50 @@
     main = freqs - 1
     owners = members * n_rcv * halves
     per = main // owners
-    assert per * owners == main
+    assert per * owners == main and halves == 2 and points == lanes
     cols = 2 * per * halves
     block = shots // (n_shot * halves)
     bf16 = functools.partial(jax.ShapeDtypeStruct, dtype=jnp.bfloat16)
     high, low = dft_tables(window, members, n_rcv, per * halves, main)
 
+    message = bf16((n_rows // LANES * (cols + 4), LANES))
     messages = call(
         functools.partial(spectra_kernel, cols),
-        (bf16((n_rows // LANES * (cols + 4), LANES)),) * members,
+        (message,) * members,
         (traces[0], high, low, trace_block.reshape(1, n_rows), trace_shot, trace_point),
         limit=56 * 1024 * 1024,
     )
-    rows = [messages[0]]
-    for d in range(1, n_shot):
-        rows.append(lax.ppermute(messages[d % members], SHOT, [(s, s ^ d) for s in range(n_shot)]))
+    near = [messages[0]]
+    for d in range(members - 1, 0, -1):
+        near.append(lax.ppermute(messages[d], "member", [(t, t ^ d) for t in range(members)]))
+    near = jnp.stack(near)
+    far = lax.ppermute(near, "group", [(g, g ^ 1) for g in range(groups)])
 
     recv = recv_panel[:main].reshape(owners, per * 2 * width, lanes)
-    recv, *rows = lax.optimization_barrier((recv, *rows))
+    recv, near = lax.optimization_barrier((recv, near))
     recv = lax.all_to_all(recv, ("member", "rcv", "surf"), split_axis=0, concat_axis=0, tiled=True)
 
-    panel = bf16((2 * per, shots, points))
-    *panels, top = call(
-        functools.partial(bin_kernel, halves, shots, points, cols, n_shot),
-        (panel,) * halves + (bf16((n_shot * halves, 2 * block, lanes)),),
-        (*rows, recv_panel[main]),
-        (
-            pltpu.VMEM((n_shot,) + rows[0].shape, jnp.bfloat16),
-            pltpu.VMEM((STACK * shots, n_rows), jnp.bfloat16),
-            pltpu.VMEM((cols + 3, shots, points), jnp.float32),
-            pltpu.VMEM((2, points, lanes), jnp.bfloat16),
-        ),
-    )
+    acc = jax.ShapeDtypeStruct((cols + 3, shots, points), jnp.float32)
+    left = pltpu.VMEM((STACK * shots, n_rows), jnp.bfloat16)
+    work = (cols + 3) * shots * points * n_rows * members
+    acc_near = call(functools.partial(near_kernel, cols), acc, (near,), (left,), flops=NEAR * work)
+    panels = call(
+        functools.partial(far_kernel, cols, halves),
+        (bf16((2 * per + 2, shots, points)),) * halves,
+        (far, acc_near, recv_panel[main]),
+        (left, pltpu.VMEM(acc.shape, jnp.float32), pltpu.VMEM((2, points, lanes), jnp.bfloat16)),
+        flops=FAR * work,
+    )
+    panels = list(panels)
     for k in range(1, halves):
         panels[k] = lax.ppermute(panels[k], "surf", [(h, h ^ k) for h in range(halves)])
     out = call(
         functools.partial(product_kernel, members, n_shot, n_rcv, halves, width),
-        bf16((n_shot * n_rcv * halves, (per + 1) * 2 * block, lanes)),
-        (*panels, recv, top),
+        bf16((n_shot * n_rcv * halves, (2 * per + 1) * block, lanes)),
+        (*panels, recv),
     )
     out = lax.all_to_all(out, SHOT + ("rcv", "surf"), split_axis=0, concat_axis=0, tiled=True)
-    return call(functools.partial(gather_kernel, per, groups), bf16((freqs, 2, block, lanes)), (out,))
+    return call(functools.partial(gather_kernel, per, groups, halves), bf16((freqs, 2, block, lanes)), (out,))
 
 
 def solution(mesh):

time: 93 us -> 87.2 us (0.938)
  starting transfers between devices: 19.3 us -> 12.6 us
  waiting for transfers between devices: 6.95 us -> 9.57 us
  blocking collectives: 34.5 us -> 32.7 us
    ppermute x7 -> x4, starting transfers between devices: 15.1 us -> 7.3 us  [the longest x3 4.55 us: local(): lax.ppermute(messages[d], 'member', [(t, t ^ d) for t in range(members)])]
    all_to_all x1, waiting for transfers between devices: 3.22 us -> 7.62 us  [local(): lax.all_to_all(recv, ('member', 'rcv', 'surf'), split_axis=0, concat_axis...]
    all_to_all x1, blocking collectives: 34.5 us -> 32.7 us  [local(): lax.all_to_all(out, SHOT + ('rcv', 'surf'), split_axis=0, concat_axis=0,...]
    ppermute x7 -> x4, waiting for transfers between devices: 2.11 us -> 0.31 us  [the longest x3 0.31 us: local(): lax.ppermute(messages[d], 'member', [(t, t ^ d) for t in range(members)])]
    all_to_all x1, starting transfers between devices: 3.85 us -> 4.84 us  [local(): lax.all_to_all(recv, ('member', 'rcv', 'surf'), split_axis=0, concat_axis...]
    pallas_call x4 -> x5, Pallas kernels: 27.9 us -> 27.8 us  [call(): pl.pallas_call(kernel, out_shape=out_shape, in_specs=[VMEM] * len(operand...]
  transfers between devices with their start and end apart: 9 -> 6, of which waited for: 3 -> 3; matrix products, arithmetic and copies ran while one was open for 4% -> 5% of each run, Pallas kernels for 26% -> 27%
where the time goes in v4:
time: 87.2 us; the launch traced here: 86.9 us
  blocking collectives  32.7 us (38%)
  Pallas kernels  27.8 us (32%)
  starting transfers between devices  12.6 us (14%)
  waiting for transfers between devices  9.57 us (11%)
  local copies, waits for them, and re-layouts  4.1 us (5%)
    all_to_all x1, blocking collectives, local(): lax.all_to_all(out, SHOT + ('rcv', 'surf'), split_axis=0, concat_axis=0,...  32.7 us
    pallas_call x5, Pallas kernels, call(): pl.pallas_call(kernel, out_shape=out_shape, in_specs=[VMEM] * len(operand...  27.8 us
    all_to_all x1, waiting for transfers between devices, local(): lax.all_to_all(recv, ('member', 'rcv', 'surf'), split_axis=0, concat_axis...  7.62 us
    all_to_all x1, starting transfers between devices, local(): lax.all_to_all(recv, ('member', 'rcv', 'surf'), split_axis=0, concat_axis...  4.84 us
    ppermute x3, starting transfers between devices, local(): lax.ppermute(messages[d], 'member', [(t, t ^ d) for t in range(members)])  4.55 us
    slice x1, local copies, waits for them, and re-layouts, local(): recv = recv_panel[:main].reshape(owners, per * 2 * width, lanes)  3.38 us
    ppermute x1, starting transfers between devices, local(): far = lax.ppermute(near, 'group', [(g, g ^ 1) for g in range(groups)])  2.75 us
  transfers between devices with their start and end apart: 6, of which 3 were waited for; matrix products, arithmetic and copies ran while one was open for 5% of the time, Pallas kernels for 27%

profile of v4, /device:TPU:0, one launch (start us, length us, event | category | flops | bytes accessed | tf_op | source)
XLA Modules:
  0.0 86.9 jit_solution(979534945347176732)
XLA Ops:
  0.0 2.3 %shard_map.73 = (bf16[288,128]{1,0:T(8,128)(2,1)}, bf16[288,128]{1,0:T(8,128)(2,1)}, bf16[288,128]{1,0:T(8,128)(2,1)}, bf16[288,128]{1,0:T(8,128)(2,1)}) custom-call(bf16[1024,256]{1,0:T(8,128)(2,1)} %bitcast.10, bf16[2,4,48,256]{3,2,1,0:T(8,128)(2,1)} %constant.4.clone.high_ref, bf16[2,4,48,256]{3,2,1,0:T(8,128)(2,1)} %constant.5.clone.low_ref, ...), custom_call_target="tpu_custom_call" | custom-call | tf_op jit(solution)/shard_map/pallas_call | solution.py:182
  2.3 4.0 %collective-permute-start = (bf16[288,128]{1,0:T(8,128)(2,1)}, bf16[288,128]{1,0:T(8,128)(2,1)S(1)}, u32[]{:S(2)}, u32[]{:S(2)}) collective-permute-start(bf16[288,128]{1,0:T(8,128)(2,1)} %get-tuple-element.14), channel_id=1, source_target_pairs={{0,12},{4,8},{8,4},{12,0},{1,13},{5,9},{9,5},{13,1},{2,14},{6,10},... | collective-permute-start | bytes 221192 | tf_op jit(solution)/shard_map/ppermute | solution.py:218
  6.2 0.4 collective-permute-start.1
  6.7 0.1 collective-permute-start.2
  6.8 0.7 slice_bitcast_fusion.own_ref
  7.5 0.0 copy-start
  7.6 3.4 %slice.6 = bf16[128,2,32,128]{3,2,1,0:T(8,128)(2,1)} slice(bf16[129,2,32,128]{3,2,1,0:T(8,128)(2,1)} %param.11), slice={[0:128], [0:2], [0:32], [0:128]} | slice | bytes 4194304 | tf_op jit(solution)/shard_map/slice | solution.py:222
  10.9 0.0 collective-permute-done
  10.9 0.0 collective-permute-done.1
  10.9 0.3 collective-permute-done.2
  11.2 0.0 copy-done
  11.3 2.8 %collective-permute-start.3 = (bf16[4,288,128]{2,1,0:T(8,128)(2,1)S(1)}, bf16[4,288,128]{2,1,0:T(8,128)(2,1)S(1)}, u32[]{:S(2)}, u32[]{:S(2)}) collective-permute-start(bf16[4,288,128]{2,1,0:T(8,128)(2,1)S(1)} %pad_maximum_fusion.rows_ref), channel_id=1, source_target_pairs={{0,16},{16,0},{1,17},{17,1},{2,18},{18,2},{3,19},{19,3},{4,20},{20... | collective-permute-start | bytes 884744 | tf_op jit(solution)/shard_map/ppermute | solution.py:220
  14.0 4.8 %all-to-all-start = ((bf16[16,512,128]{2,1,0:T(8,128)(2,1)}), bf16[16,512,128]{2,1,0:T(8,128)(2,1)S(1)}, u32[]{:S(2)}, u32[]{:S(2)}) async-start(bf16[16,512,128]{2,1,0:T(8,128)(2,1)} %bitcast.9), calls=%async_computation | async-start | bytes 4194304 | tf_op jit(solution)/shard_map/all_to_all | solution.py:224
  18.9 11.8 %shard_map.74.near_ref = f32[35,128,128]{2,1,0:T(8,128)S(1)} custom-call(bf16[4,288,128]{2,1,0:T(8,128)(2,1)S(1)} %pad_maximum_fusion.rows_ref), custom_call_target="tpu_custom_call" | custom-call | flops 28185722880 | tf_op jit(solution)/shard_map/pallas_call | solution.py:182
  30.7 0.0 collective-permute-done.3.rows_ref
  30.7 12.1 %shard_map.75 = (bf16[18,128,128]{2,1,0:T(8,128)(2,1)S(1)}, bf16[18,128,128]{2,1,0:T(8,128)(2,1)S(1)}) custom-call(bf16[4,288,128]{2,1,0:T(8,128)(2,1)S(1)} %collective-permute-done.3.rows_ref, f32[35,128,128]{2,1,0:T(8,128)S(1)} %shard_map.74.near_ref, bf16[2,32,128]{2,1,0:T(8,128)(2,1)S(1)} %slice_bitcast_fusion.own_ref), custom_call_target="tpu_custom_call" | custom-call | flops 28185722880 | tf_op jit(solution)/shard_map/pallas_call | solution.py:182
  42.8 0.5 collective-permute-start.4
  43.3 1.6 %collective-permute-done.4.refs_1_ = bf16[18,128,128]{2,1,0:T(8,128)(2,1)S(1)} collective-permute-done((bf16[18,128,128]{2,1,0:T(8,128)(2,1)S(1)}, bf16[18,128,128]{2,1,0:T(8,128)(2,1)S(1)}, u32[]{:S(2)}, u32[]{:S(2)}) %collective-permute-start.4) | collective-permute-done | bytes 589856 | tf_op jit(solution)/shard_map/ppermute | solution.py:239
  44.9 7.6 %all-to-all-done.refs_2_ = bf16[16,512,128]{2,1,0:T(8,128)(2,1)S(1)} async-done(((bf16[16,512,128]{2,1,0:T(8,128)(2,1)}), bf16[16,512,128]{2,1,0:T(8,128)(2,1)S(1)}, u32[]{:S(2)}, u32[]{:S(2)}) %all-to-all-start) | async-done | bytes 2097184 | tf_op jit(solution)/shard_map/all_to_all | solution.py:224
  52.5 0.7 shard_map.76
  53.3 32.7 %all_to_all.10.got_ref = bf16[32,136,128]{2,1,0:T(8,128)(2,1)S(1)} all-to-all(bf16[32,136,128]{2,1,0:T(8,128)(2,1)S(1)} %shard_map.76), channel_id=1, replica_groups=mesh['group'=2,'member'=4,'rcv'=2,'surf'=2] {'group','member','rcv','surf'}, dimensions={0} | all-to-all | bytes 2228224 | tf_op jit(solution)/shard_map/all_to_all | solution.py:245
  85.9 0.9 %shard_map.77 = bf16[129,2,8,128]{3,2,1,0:T(8,128)(2,1)} custom-call(bf16[32,136,128]{2,1,0:T(8,128)(2,1)S(1)} %all_to_all.10.got_ref), custom_call_target="tpu_custom_call" | custom-call | tf_op jit(solution)/shard_map/pallas_call | solution.py:182
  (1 shorter events, 0.0 us)
Async XLA Ops:
  2.3 8.7 %collective-permute-start = (bf16[288,128]{1,0:T(8,128)(2,1)}, bf16[288,128]{1,0:T(8,128)(2,1)S(1)}, u32[]{:S(2)}, u32[]{:S(2)}) collective-permute-start(bf16[288,128]{1,0:T(8,128)(2,1)} %get-tuple-element.14), channel_id=1, source_target_pairs={{0,12},{4,8},{8,4},{12,0},{1,13},{5,9},{9,5},{13,1},{2,14},{6,10},... | collective-permute-start | bytes 221192 | tf_op jit(solution)/shard_map/ppermute | solution.py:218
  6.2 4.7 %collective-permute-start.1 = (bf16[288,128]{1,0:T(8,128)(2,1)}, bf16[288,128]{1,0:T(8,128)(2,1)S(1)}, u32[]{:S(2)}, u32[]{:S(2)}) collective-permute-start(bf16[288,128]{1,0:T(8,128)(2,1)} %get-tuple-element.15), channel_id=1, source_target_pairs={{0,8},{4,12},{8,0},{12,4},{1,9},{5,13},{9,1},{13,5},{2,10},{6,14},... | collective-permute-start | bytes 221192 | tf_op jit(solution)/shard_map/ppermute | solution.py:218
  6.7 4.6 %collective-permute-start.2 = (bf16[288,128]{1,0:T(8,128)(2,1)}, bf16[288,128]{1,0:T(8,128)(2,1)S(1)}, u32[]{:S(2)}, u32[]{:S(2)}) collective-permute-start(bf16[288,128]{1,0:T(8,128)(2,1)} %get-tuple-element.16), channel_id=1, source_target_pairs={{0,4},{4,0},{8,12},{12,8},{1,5},{5,1},{9,13},{13,9},{2,6},{6,2},{1... | collective-permute-start | bytes 221192 | tf_op jit(solution)/shard_map/ppermute | solution.py:218
  7.5 3.7 %copy-start = (bf16[288,128]{1,0:T(8,128)(2,1)S(1)}, bf16[288,128]{1,0:T(8,128)(2,1)}, u32[]{:S(2)}) copy-start(bf16[288,128]{1,0:T(8,128)(2,1)} %get-tuple-element.13) | copy-start | bytes 221188
  11.3 19.4 %collective-permute-start.3 = (bf16[4,288,128]{2,1,0:T(8,128)(2,1)S(1)}, bf16[4,288,128]{2,1,0:T(8,128)(2,1)S(1)}, u32[]{:S(2)}, u32[]{:S(2)}) collective-permute-start(bf16[4,288,128]{2,1,0:T(8,128)(2,1)S(1)} %pad_maximum_fusion.rows_ref), channel_id=1, source_target_pairs={{0,16},{16,0},{1,17},{17,1},{2,18},{18,2},{3,19},{19,3},{4,20},{20... | collective-permute-start | bytes 884744 | tf_op jit(solution)/shard_map/ppermute | solution.py:220
  14.0 38.5 %all-to-all-start = ((bf16[16,512,128]{2,1,0:T(8,128)(2,1)}), bf16[16,512,128]{2,1,0:T(8,128)(2,1)S(1)}, u32[]{:S(2)}, u32[]{:S(2)}) async-start(bf16[16,512,128]{2,1,0:T(8,128)(2,1)} %bitcast.9), calls=%async_computation | async-start | bytes 4194304 | tf_op jit(solution)/shard_map/all_to_all | solution.py:224
  42.8 2.1 %collective-permute-start.4 = (bf16[18,128,128]{2,1,0:T(8,128)(2,1)S(1)}, bf16[18,128,128]{2,1,0:T(8,128)(2,1)S(1)}, u32[]{:S(2)}, u32[]{:S(2)}) collective-permute-start(bf16[18,128,128]{2,1,0:T(8,128)(2,1)S(1)} %get-tuple-element.19), channel_id=1, source_target_pairs={{0,1},{1,0},{2,3},{3,2},{4,5},{5,4},{6,7},{7,6},{8,9},{9,8},{10,11... | collective-permute-start | bytes 1769480 | tf_op jit(solution)/shard_map/ppermute | solution.py:239

commit v5 on v4

--- a/solution.py
+++ b/solution.py
@@ -17,9 +17,14 @@
 
 
 GROUPS = 2
-NEAR, FAR = 12, 12
-STACK = 5
+HEAD = 1
+HEAD_COST, NEAR_COST, FAR_COST = 48, 24, 24
+STACK = 7
 SHOT = ("group", "member")
+
+
+def share_of(group, member, members):
+    return member ^ (group * (members // 2))
 
 
 def dft_tables(window, members, n_rcv, per, top):
@@ -45,9 +50,9 @@
 
 def spectra_kernel(cols, x_ref, high_ref, low_ref, block_ref, shot_ref, point_ref, *out_refs):
     x = x_ref[...]
-    mine, member = lax.axis_index("rcv"), lax.axis_index("member")
+    mine, first = lax.axis_index("rcv"), share_of(lax.axis_index("group"), lax.axis_index("member"), high_ref.shape[1])
     slots = high_ref.shape[2]
-    y = nt(jnp.concatenate([ref[mine, member ^ d] for ref in (high_ref, low_ref) for d in range(len(out_refs))], axis=0), x)
+    y = nt(jnp.concatenate([ref[mine, first ^ d] for ref in (high_ref, low_ref) for d in range(len(out_refs))], axis=0), x)
     y = y[: slots * len(out_refs)] + y[slots * len(out_refs) :]
     shot = (block_ref[...] * SHOTS_PER_INDEX + shot_ref[...]).astype(jnp.float32)
     point = point_ref[...].astype(jnp.float32)
@@ -59,7 +64,7 @@
         out_ref[...] = jnp.concatenate(pieces, axis=0).astype(jnp.bfloat16)
 
 
-def add_rows(cols, rows_ref, left_ref, acc_ref):
+def add_rows(cols, rows_ref, first_source, last_source, left_ref, acc_ref):
     _, shots, points = acc_ref.shape
     slots = cols + 4
     parts = rows_ref.shape[1] // slots
@@ -87,22 +92,24 @@
             acc_ref[first : first + len(stack)] += got.reshape(len(stack), shots, points)
         return carry
 
-    lax.fori_loop(0, rows_ref.shape[0], step, 0)
-
-
-def near_kernel(cols, rows_ref, acc_ref, left_ref):
-    acc_ref[...] = jnp.zeros_like(acc_ref)
-    add_rows(cols, rows_ref, left_ref, acc_ref)
-
-
-def far_kernel(cols, halves, rows_ref, near_ref, own_ref, *refs):
-    panel_refs, (left_ref, acc_ref, pad_ref) = refs[:halves], refs[halves:]
+    lax.fori_loop(first_source, last_source, step, 0)
+
+
+def near_kernel(cols, first, last, rows_ref, *refs):
+    *before, acc_ref, left_ref = refs
+    acc_ref[...] = before[0][...] if before else jnp.zeros_like(acc_ref)
+    add_rows(cols, rows_ref, first, last, left_ref, acc_ref)
+
+
+def far_kernel(cols, halves, outer_ref, inner_ref, near_ref, own_ref, *refs):
+    panel_refs, (rows_ref, left_ref, acc_ref, pad_ref) = refs[:halves], refs[halves:]
     width = own_ref.shape[1]
     member, own_half = lax.axis_index("member"), lax.axis_index("surf")
     pad_ref[...] = jnp.zeros_like(pad_ref)
     pad_ref[:, pl.ds(pl.multiple_of(member * width, width), width), :] = own_ref[...]
     acc_ref[...] = near_ref[...]
-    add_rows(cols, rows_ref, left_ref, acc_ref)
+    rows_ref[...] = outer_ref[...] + inner_ref[...]
+    add_rows(cols, rows_ref, 0, rows_ref.shape[0], left_ref, acc_ref)
     scale = 1.0 / jnp.maximum(acc_ref[cols + 2], 1.0)
     each = cols // halves
     for k, ref in enumerate(panel_refs):
@@ -171,8 +178,9 @@
     for w in range(each):
         value = jnp.zeros((rows, got_ref.shape[2]), jnp.float32)
         for g in range(groups):
-            value = value + got_ref[g * each + w, :rows, :].astype(jnp.float32)
-            tops[w % halves] = tops[w % halves] + got_ref[g * each + w, rows:, :].astype(jnp.float32)
+            source = g * each + share_of(g, w, each)
+            value = value + got_ref[source, :rows, :].astype(jnp.float32)
+            tops[w % halves] = tops[w % halves] + got_ref[source, rows:, :].astype(jnp.float32)
         out_ref[w * per : (w + 1) * per] = value.reshape((per,) + out_ref.shape[1:]).astype(jnp.bfloat16)
     for c in range(halves):
         out_ref[each * per, c] = tops[c].astype(jnp.bfloat16)
@@ -217,22 +225,30 @@
     for d in range(members - 1, 0, -1):
         near.append(lax.ppermute(messages[d], "member", [(t, t ^ d) for t in range(members)]))
     near = jnp.stack(near)
-    far = lax.ppermute(near, "group", [(g, g ^ 1) for g in range(groups)])
-
-    recv = recv_panel[:main].reshape(owners, per * 2 * width, lanes)
+    pairs = [(m, members + share_of(1, m, members)) for m in range(members)]
+    outer, inner = (chosen + [(b, a) for a, b in chosen] for chosen in (pairs[: members // 2], pairs[members // 2 :]))
+    outer = lax.ppermute(near, SHOT, outer)
+
+    share = main // 2
+    swap = lax.axis_index("group") * share
+    recv = [lax.dynamic_slice_in_dim(recv_panel, start, share, 0) for start in (swap, share - swap)]
+    recv = jnp.concatenate(recv, axis=0).reshape(owners, per * 2 * width, lanes)
     recv, near = lax.optimization_barrier((recv, near))
     recv = lax.all_to_all(recv, ("member", "rcv", "surf"), split_axis=0, concat_axis=0, tiled=True)
 
     acc = jax.ShapeDtypeStruct((cols + 3, shots, points), jnp.float32)
     left = pltpu.VMEM((STACK * shots, n_rows), jnp.bfloat16)
-    work = (cols + 3) * shots * points * n_rows * members
-    acc_near = call(functools.partial(near_kernel, cols), acc, (near,), (left,), flops=NEAR * work)
+    work = (cols + 3) * shots * points * n_rows
+    acc_near = call(functools.partial(near_kernel, cols, 0, HEAD), acc, (near,), (left,), flops=HEAD_COST * work)
+    tied, acc_near = lax.optimization_barrier((near, acc_near))
+    inner = lax.ppermute(tied, SHOT, inner)
+    acc_near = call(functools.partial(near_kernel, cols, HEAD, members), acc, (near, acc_near), (left,), flops=NEAR_COST * work)
     panels = call(
         functools.partial(far_kernel, cols, halves),
         (bf16((2 * per + 2, shots, points)),) * halves,
-        (far, acc_near, recv_panel[main]),
-        (left, pltpu.VMEM(acc.shape, jnp.float32), pltpu.VMEM((2, points, lanes), jnp.bfloat16)),
-        flops=FAR * work,
+        (outer, inner, acc_near, recv_panel[main]),
+        (pltpu.VMEM(near.shape, jnp.bfloat16), left, pltpu.VMEM(acc.shape, jnp.float32), pltpu.VMEM((2, points, lanes), jnp.bfloat16)),
+        flops=FAR_COST * work,
     )
     panels = list(panels)
     for k in range(1, halves):

time: 87.2 us -> 87 us (level)
  waiting for transfers between devices: 9.57 us -> 4.05 us
  starting transfers between devices: 12.6 us -> 15.3 us
  other arithmetic: 0.04 us -> 1.55 us
  blocking collectives: 32.7 us -> 34.2 us
  local copies, waits for them, and re-layouts: 4.1 us -> 2.69 us
  Pallas kernels: 27.8 us -> 28.9 us
    all_to_all x1, waiting for transfers between devices: 7.62 us -> 2.22 us  [local(): lax.all_to_all(recv, ('member', 'rcv', 'surf'), split_axis=0, concat_axis...]
    ppermute x1 -> x2, starting transfers between devices: 2.75 us -> 6.39 us  [the longest x1 5.71 us: local(): outer = lax.ppermute(near, SHOT, outer)]
    slice x1 -> x0, local copies, waits for them, and re-layouts: 3.38 us -> none  [local(): recv = recv_panel[:main].reshape(owners, per * 2 * width, lanes)]
    dynamic_slice x0 -> x1, local copies, waits for them, and re-layouts: none -> 1.96 us  [local(): lax.dynamic_slice_in_dim(recv_panel, start, share, 0)]
    all_to_all x1, blocking collectives: 32.7 us -> 34.2 us  [local(): lax.all_to_all(out, SHOT + ('rcv', 'surf'), split_axis=0, concat_axis=0,...]
    concatenate x0 -> x1, other arithmetic: none -> 1.51 us  [local(): recv = jnp.concatenate(recv, axis=0).reshape(owners, per * 2 * width, lanes)]
    pallas_call x5 -> x6, Pallas kernels: 27.8 us -> 28.9 us  [call(): pl.pallas_call(kernel, out_shape=out_shape, in_specs=[VMEM] * len(operand...]
    all_to_all x1, starting transfers between devices: 4.84 us -> 3.84 us  [local(): lax.all_to_all(recv, ('member', 'rcv', 'surf'), split_axis=0, concat_axis...]
  transfers between devices with their start and end apart: 6 -> 7, of which waited for: 3 -> 3; matrix products, arithmetic and copies ran while one was open for 5% -> 5% of each run, Pallas kernels for 27% -> 29%
where the time goes in v5:
time: 87 us; the launch traced here: 86.7 us
  blocking collectives  34.2 us (39%)
  Pallas kernels  28.9 us (33%)
  starting transfers between devices  15.3 us (18%)
  waiting for transfers between devices  4.05 us (5%)
  local copies, waits for them, and re-layouts  2.69 us (3%)
  other arithmetic  1.55 us (2%)
    all_to_all x1, blocking collectives, local(): lax.all_to_all(out, SHOT + ('rcv', 'surf'), split_axis=0, concat_axis=0,...  34.2 us
    pallas_call x6, Pallas kernels, call(): pl.pallas_call(kernel, out_shape=out_shape, in_specs=[VMEM] * len(operand...  28.9 us
    ppermute x1, starting transfers between devices, local(): outer = lax.ppermute(near, SHOT, outer)  5.71 us
    ppermute x3, starting transfers between devices, local(): lax.ppermute(messages[d], 'member', [(t, t ^ d) for t in range(members)])  4.56 us
    all_to_all x1, starting transfers between devices, local(): lax.all_to_all(recv, ('member', 'rcv', 'surf'), split_axis=0, concat_axis...  3.84 us
    all_to_all x1, waiting for transfers between devices, local(): lax.all_to_all(recv, ('member', 'rcv', 'surf'), split_axis=0, concat_axis...  2.22 us
    dynamic_slice x1, local copies, waits for them, and re-layouts, local(): lax.dynamic_slice_in_dim(recv_panel, start, share, 0)  1.96 us
  transfers between devices with their start and end apart: 7, of which 3 were waited for; matrix products, arithmetic and copies ran while one was open for 5% of the time, Pallas kernels for 29%

profile of v5, /device:TPU:0, one launch (start us, length us, event | category | flops | bytes accessed | tf_op | source)
XLA Modules:
  0.0 86.7 jit_solution(12295636420092826618)
XLA Ops:
  0.0 2.3 %shard_map.73 = (bf16[288,128]{1,0:T(8,128)(2,1)}, bf16[288,128]{1,0:T(8,128)(2,1)}, bf16[288,128]{1,0:T(8,128)(2,1)}, bf16[288,128]{1,0:T(8,128)(2,1)}) custom-call(bf16[1024,256]{1,0:T(8,128)(2,1)} %bitcast.10, bf16[2,4,48,256]{3,2,1,0:T(8,128)(2,1)} %constant.18.clone.high_ref, bf16[2,4,48,256]{3,2,1,0:T(8,128)(2,1)} %constant.19.clone.low_ref, ...), custom_call_target="tpu_custom_call" | custom-call | tf_op jit(solution)/shard_map/pallas_call | solution.py:190
  2.3 4.0 %collective-permute-start = (bf16[288,128]{1,0:T(8,128)(2,1)}, bf16[288,128]{1,0:T(8,128)(2,1)S(1)}, u32[]{:S(2)}, u32[]{:S(2)}) collective-permute-start(bf16[288,128]{1,0:T(8,128)(2,1)} %get-tuple-element.16), channel_id=1, source_target_pairs={{0,12},{4,8},{8,4},{12,0},{1,13},{5,9},{9,5},{13,1},{2,14},{6,10},... | collective-permute-start | bytes 221192 | tf_op jit(solution)/shard_map/ppermute | solution.py:226
  6.2 0.4 collective-permute-start.1
  6.7 0.2 collective-permute-start.2
  6.8 0.7 slice_bitcast_fusion.own_ref
  7.5 2.0 %constant_dynamic-slice_fusion.1 = (bf16[64,2,32,128]{3,2,1,0:T(8,128)(2,1)S(1)}, bf16[64,2,32,128]{3,2,1,0:T(8,128)(2,1)S(1)}) fusion(bf16[129,2,32,128]{3,2,1,0:T(8,128)(2,1)} %param.11, s32[]{:T(128)S(6)} %select_n.6, s32[]{:T(128)S(6)} %select_n.7), kind=kLoop, calls=%fused_computation.4 | loop fusion | bytes 4194312 | tf_op jit(solution)/shard_map/dynamic_slice | solution.py:234
  9.5 0.0 copy-start
  9.5 1.5 %pad_maximum_fusion = bf16[128,2,32,128]{3,2,1,0:T(8,128)(2,1)} fusion(bf16[64,2,32,128]{3,2,1,0:T(8,128)(2,1)S(1)} %get-tuple-element.26, bf16[64,2,32,128]{3,2,1,0:T(8,128)(2,1)S(1)} %get-tuple-element.25), kind=kLoop, calls=%fused_computation | loop fusion | flops 1048576 | bytes 4194304 | tf_op jit(solution)/shard_map/concatenate | solution.py:235
  11.0 0.0 collective-permute-done
  11.0 0.0 collective-permute-done.1
  11.0 0.2 collective-permute-done.2
  11.2 0.0 copy-done
  11.3 5.7 %collective-permute-start.3 = (bf16[4,288,128]{2,1,0:T(8,128)(2,1)S(1)}, bf16[4,288,128]{2,1,0:T(8,128)(2,1)S(1)}, u32[]{:S(2)}, u32[]{:S(2)}) collective-permute-start(bf16[4,288,128]{2,1,0:T(8,128)(2,1)S(1)} %pad_maximum_fusion.1.rows_ref), channel_id=1, source_target_pairs={{0,24},{4,28},{24,0},{28,4},{1,25},{5,29},{25,1},{29,5},{2,26},{6,... | collective-permute-start | bytes 884744 | tf_op jit(solution)/shard_map/ppermute | solution.py:230
  17.0 3.8 %all-to-all-start = ((bf16[16,512,128]{2,1,0:T(8,128)(2,1)}), bf16[16,512,128]{2,1,0:T(8,128)(2,1)S(1)}, u32[]{:S(2)}, u32[]{:S(2)}) async-start(bf16[16,512,128]{2,1,0:T(8,128)(2,1)} %bitcast.9), calls=%async_computation | async-start | bytes 4194304 | tf_op jit(solution)/shard_map/all_to_all | solution.py:237
  20.8 3.0 %shard_map.74.refs_0_ = f32[35,128,128]{2,1,0:T(8,128)S(1)} custom-call(bf16[4,288,128]{2,1,0:T(8,128)(2,1)S(1)} %pad_maximum_fusion.1.rows_ref), custom_call_target="tpu_custom_call" | custom-call | flops 28185722880 | tf_op jit(solution)/shard_map/pallas_call | solution.py:190
  23.9 0.7 collective-permute-start.4
  24.5 9.3 %shard_map.75.near_ref = f32[35,128,128]{2,1,0:T(8,128)S(1)} custom-call(bf16[4,288,128]{2,1,0:T(8,128)(2,1)S(1)} %pad_maximum_fusion.1.rows_ref, f32[35,128,128]{2,1,0:T(8,128)S(1)} %shard_map.74.refs_0_), custom_call_target="tpu_custom_call" | custom-call | flops 14092861440 | tf_op jit(solution)/shard_map/pallas_call | solution.py:190
  33.8 0.0 collective-permute-done.4.inner_ref
  33.8 0.0 collective-permute-done.3.outer_ref
  33.8 12.7 %shard_map.76 = (bf16[18,128,128]{2,1,0:T(8,128)(2,1)S(1)}, bf16[18,128,128]{2,1,0:T(8,128)(2,1)S(1)}) custom-call(bf16[4,288,128]{2,1,0:T(8,128)(2,1)S(1)} %collective-permute-done.3.outer_ref, bf16[4,288,128]{2,1,0:T(8,128)(2,1)S(1)} %collective-permute-done.4.inner_ref, f32[35,128,128]{2,1,0:T(8,128)S(1)} %shard_map.75.near_ref, ...), custom_call_target="tpu_custom_call" | custom-call | flops 14092861440 | tf_op jit(solution)/shard_map/pallas_call | solution.py:190
  46.5 0.5 collective-permute-start.5
  47.0 1.6 %collective-permute-done.5.refs_1_ = bf16[18,128,128]{2,1,0:T(8,128)(2,1)S(1)} collective-permute-done((bf16[18,128,128]{2,1,0:T(8,128)(2,1)S(1)}, bf16[18,128,128]{2,1,0:T(8,128)(2,1)S(1)}, u32[]{:S(2)}, u32[]{:S(2)}) %collective-permute-start.5) | collective-permute-done | bytes 589856 | tf_op jit(solution)/shard_map/ppermute | solution.py:255
  48.6 2.2 %all-to-all-done.refs_2_ = bf16[16,512,128]{2,1,0:T(8,128)(2,1)S(1)} async-done(((bf16[16,512,128]{2,1,0:T(8,128)(2,1)}), bf16[16,512,128]{2,1,0:T(8,128)(2,1)S(1)}, u32[]{:S(2)}, u32[]{:S(2)}) %all-to-all-start) | async-done | bytes 2097184 | tf_op jit(solution)/shard_map/all_to_all | solution.py:237
  50.8 0.7 shard_map.77
  51.6 34.2 %all_to_all.10.got_ref = bf16[32,136,128]{2,1,0:T(8,128)(2,1)S(1)} all-to-all(bf16[32,136,128]{2,1,0:T(8,128)(2,1)S(1)} %shard_map.77), channel_id=1, replica_groups=mesh['group'=2,'member'=4,'rcv'=2,'surf'=2] {'group','member','rcv','surf'}, dimensions={0} | all-to-all | bytes 2228224 | tf_op jit(solution)/shard_map/all_to_all | solution.py:261
  85.7 0.9 %shard_map.78 = bf16[129,2,8,128]{3,2,1,0:T(8,128)(2,1)} custom-call(bf16[32,136,128]{2,1,0:T(8,128)(2,1)S(1)} %all_to_all.10.got_ref), custom_call_target="tpu_custom_call" | custom-call | tf_op jit(solution)/shard_map/pallas_call | solution.py:190
  (1 shorter events, 0.0 us)
Async XLA Ops:
  2.3 8.8 %collective-permute-start = (bf16[288,128]{1,0:T(8,128)(2,1)}, bf16[288,128]{1,0:T(8,128)(2,1)S(1)}, u32[]{:S(2)}, u32[]{:S(2)}) collective-permute-start(bf16[288,128]{1,0:T(8,128)(2,1)} %get-tuple-element.16), channel_id=1, source_target_pairs={{0,12},{4,8},{8,4},{12,0},{1,13},{5,9},{9,5},{13,1},{2,14},{6,10},... | collective-permute-start | bytes 221192 | tf_op jit(solution)/shard_map/ppermute | solution.py:226
  6.2 4.8 %collective-permute-start.1 = (bf16[288,128]{1,0:T(8,128)(2,1)}, bf16[288,128]{1,0:T(8,128)(2,1)S(1)}, u32[]{:S(2)}, u32[]{:S(2)}) collective-permute-start(bf16[288,128]{1,0:T(8,128)(2,1)} %get-tuple-element.17), channel_id=1, source_target_pairs={{0,8},{4,12},{8,0},{12,4},{1,9},{5,13},{9,1},{13,5},{2,10},{6,14},... | collective-permute-start | bytes 221192 | tf_op jit(solution)/shard_map/ppermute | solution.py:226
  6.7 4.6 %collective-permute-start.2 = (bf16[288,128]{1,0:T(8,128)(2,1)}, bf16[288,128]{1,0:T(8,128)(2,1)S(1)}, u32[]{:S(2)}, u32[]{:S(2)}) collective-permute-start(bf16[288,128]{1,0:T(8,128)(2,1)} %get-tuple-element.18), channel_id=1, source_target_pairs={{0,4},{4,0},{8,12},{12,8},{1,5},{5,1},{9,13},{13,9},{2,6},{6,2},{1... | collective-permute-start | bytes 221192 | tf_op jit(solution)/shard_map/ppermute | solution.py:226
  9.5 1.7 %copy-start = (bf16[288,128]{1,0:T(8,128)(2,1)S(1)}, bf16[288,128]{1,0:T(8,128)(2,1)}, u32[]{:S(2)}) copy-start(bf16[288,128]{1,0:T(8,128)(2,1)} %get-tuple-element.15) | copy-start | bytes 221188
  11.3 22.5 %collective-permute-start.3 = (bf16[4,288,128]{2,1,0:T(8,128)(2,1)S(1)}, bf16[4,288,128]{2,1,0:T(8,128)(2,1)S(1)}, u32[]{:S(2)}, u32[]{:S(2)}) collective-permute-start(bf16[4,288,128]{2,1,0:T(8,128)(2,1)S(1)} %pad_maximum_fusion.1.rows_ref), channel_id=1, source_target_pairs={{0,24},{4,28},{24,0},{28,4},{1,25},{5,29},{25,1},{29,5},{2,26},{6,... | collective-permute-start | bytes 884744 | tf_op jit(solution)/shard_map/ppermute | solution.py:230
  17.0 33.8 %all-to-all-start = ((bf16[16,512,128]{2,1,0:T(8,128)(2,1)}), bf16[16,512,128]{2,1,0:T(8,128)(2,1)S(1)}, u32[]{:S(2)}, u32[]{:S(2)}) async-start(bf16[16,512,128]{2,1,0:T(8,128)(2,1)} %bitcast.9), calls=%async_computation | async-start | bytes 4194304 | tf_op jit(solution)/shard_map/all_to_all | solution.py:237
  23.9 10.0 %collective-permute-start.4 = (bf16[4,288,128]{2,1,0:T(8,128)(2,1)S(1)}, bf16[4,288,128]{2,1,0:T(8,128)(2,1)S(1)}, u32[]{:S(2)}, u32[]{:S(2)}) collective-permute-start(bf16[4,288,128]{2,1,0:T(8,128)(2,1)S(1)} %pad_maximum_fusion.1.rows_ref), channel_id=1, source_target_pairs={{8,16},{12,20},{16,8},{20,12},{9,17},{13,21},{17,9},{21,13},{10,18... | collective-permute-start | bytes 884744 | tf_op jit(solution)/shard_map/ppermute | solution.py:244
  46.5 2.1 %collective-permute-start.5 = (bf16[18,128,128]{2,1,0:T(8,128)(2,1)S(1)}, bf16[18,128,128]{2,1,0:T(8,128)(2,1)S(1)}, u32[]{:S(2)}, u32[]{:S(2)}) collective-permute-start(bf16[18,128,128]{2,1,0:T(8,128)(2,1)S(1)} %get-tuple-element.23), channel_id=1, source_target_pairs={{0,1},{1,0},{2,3},{3,2},{4,5},{5,4},{6,7},{7,6},{8,9},{9,8},{10,11... | collective-permute-start | bytes 1769480 | tf_op jit(solution)/shard_map/ppermute | solution.py:255

commit v6 on v5

--- a/solution.py
+++ b/solution.py
@@ -18,7 +18,7 @@
 
 GROUPS = 2
 HEAD = 1
-HEAD_COST, NEAR_COST, FAR_COST = 48, 24, 24
+HEAD_COST, NEAR_COST, FAR_COST = 48, 24, 12
 STACK = 7
 SHOT = ("group", "member")
 
@@ -27,17 +27,19 @@
     return member ^ (group * (members // 2))
 
 
-def dft_tables(window, members, n_rcv, per, top):
+def dft_tables(window, members, n_rcv, halves, per, top):
     slots = -(-(2 * per + 4) // 16) * 16
     n = np.arange(window, dtype=np.int64)
-    table = np.zeros((n_rcv, members, slots, window), np.float64)
-    for r in range(n_rcv):
-        for t in range(members):
-            first = (t * n_rcv + r) * per
-            for j, f in enumerate(list(range(first, first + per)) + [top]):
-                angle = (n * f % window) * (2.0 * math.pi / window)
-                table[r, t, 2 * j] = np.cos(angle)
-                table[r, t, 2 * j + 1] = -np.sin(angle)
+    table = np.zeros((halves, n_rcv, members, slots, window), np.float64)
+    share = per // halves
+    for h, r, t in np.ndindex(halves, n_rcv, members):
+        first = (t * n_rcv + r) * per
+        freqs = [first + (h ^ k) * share + j for k in range(halves) for j in range(share)] + [top]
+        for j, f in enumerate(freqs):
+            angle = (n * f % window) * (2.0 * math.pi / window)
+            table[h, r, t, 2 * j] = np.cos(angle)
+            table[h, r, t, 2 * j + 1] = -np.sin(angle)
+    table = table.reshape(halves * n_rcv, members, slots, window)
     table = (table / math.sqrt(window)).astype(np.float32)
     high = table.astype(jnp.bfloat16)
     low = (table - high.astype(np.float32)).astype(jnp.bfloat16)
@@ -50,7 +52,8 @@
 
 def spectra_kernel(cols, x_ref, high_ref, low_ref, block_ref, shot_ref, point_ref, *out_refs):
     x = x_ref[...]
-    mine, first = lax.axis_index("rcv"), share_of(lax.axis_index("group"), lax.axis_index("member"), high_ref.shape[1])
+    mine = lax.axis_index("surf") * lax.axis_size("rcv") + lax.axis_index("rcv")
+    first = share_of(lax.axis_index("group"), lax.axis_index("member"), high_ref.shape[1])
     slots = high_ref.shape[2]
     y = nt(jnp.concatenate([ref[mine, first ^ d] for ref in (high_ref, low_ref) for d in range(len(out_refs))], axis=0), x)
     y = y[: slots * len(out_refs)] + y[slots * len(out_refs) :]
@@ -64,7 +67,9 @@
         out_ref[...] = jnp.concatenate(pieces, axis=0).astype(jnp.bfloat16)
 
 
-def add_rows(cols, rows_ref, first_source, last_source, left_ref, acc_ref):
+def add_rows(cols, rows_ref, first_source, last_source, left_ref, acc_ref, low=0, high=None):
+    high = cols + 3 if high is None else high
+    chosen = (list(range(cols + 2)) + [None])[:high]
     _, shots, points = acc_ref.shape
     slots = cols + 4
     parts = rows_ref.shape[1] // slots
@@ -75,12 +80,10 @@
         ids = [rows_ref[source, j * slots + slot : j * slots + slot + 1, :] for j in range(parts)]
         return [jnp.where(grid == i.astype(jnp.float32) - first, 1.0, 0.0).astype(jnp.bfloat16) for i in ids]
 
-    chosen = list(range(cols + 2)) + [None]
-
     def step(source, carry):
         shot_hit = hits(source, shots, cols + 2, 0.0)
         point_hit = jnp.concatenate(hits(source, points, cols + 3, (group * points).astype(jnp.float32)), axis=1)
-        for first in range(0, len(chosen), STACK):
+        for first in range(low, high, STACK):
             stack = chosen[first : first + STACK]
             for i, slot in enumerate(stack):
                 for j in range(parts):
@@ -101,28 +104,32 @@
     add_rows(cols, rows_ref, first, last, left_ref, acc_ref)
 
 
-def far_kernel(cols, halves, outer_ref, inner_ref, near_ref, own_ref, *refs):
-    panel_refs, (rows_ref, left_ref, acc_ref, pad_ref) = refs[:halves], refs[halves:]
+def far_kernel(cols, outer_ref, inner_ref, near_ref, own_ref, panel_ref, scale_ref, all_ref, left_ref, acc_ref, pad_ref):
+    each = cols // 2
     width = own_ref.shape[1]
-    member, own_half = lax.axis_index("member"), lax.axis_index("surf")
     pad_ref[...] = jnp.zeros_like(pad_ref)
-    pad_ref[:, pl.ds(pl.multiple_of(member * width, width), width), :] = own_ref[...]
+    pad_ref[:, pl.ds(pl.multiple_of(lax.axis_index("member") * width, width), width), :] = own_ref[...]
     acc_ref[...] = near_ref[...]
-    rows_ref[...] = outer_ref[...] + inner_ref[...]
-    add_rows(cols, rows_ref, 0, rows_ref.shape[0], left_ref, acc_ref)
+    all_ref[...] = outer_ref[...] + inner_ref[...]
+    add_rows(cols, all_ref, 0, all_ref.shape[0], left_ref, acc_ref, low=each)
     scale = 1.0 / jnp.maximum(acc_ref[cols + 2], 1.0)
-    each = cols // halves
-    for k, ref in enumerate(panel_refs):
-        for c in range(each):
-            ref[c] = (acc_ref[(own_half ^ k) * each + c] * scale).astype(jnp.bfloat16)
+    scale_ref[...] = scale
+    for c in range(each):
+        panel_ref[c] = (acc_ref[each + c] * scale).astype(jnp.bfloat16)
     real = (acc_ref[cols] * scale).astype(jnp.bfloat16)
     imag = (acc_ref[cols + 1] * scale).astype(jnp.bfloat16)
     dot = functools.partial(jnp.dot, preferred_element_type=jnp.float32)
-    out_real = dot(real, pad_ref[0]) - dot(imag, pad_ref[1])
-    out_imag = dot(real, pad_ref[1]) + dot(imag, pad_ref[0])
-    for ref in panel_refs:
-        ref[each] = out_real.astype(jnp.bfloat16)
-        ref[each + 1] = out_imag.astype(jnp.bfloat16)
+    panel_ref[each] = (dot(real, pad_ref[0]) - dot(imag, pad_ref[1])).astype(jnp.bfloat16)
+    panel_ref[each + 1] = (dot(real, pad_ref[1]) + dot(imag, pad_ref[0])).astype(jnp.bfloat16)
+
+
+def own_kernel(cols, all_ref, near_ref, sent_ref, scale_ref, panel_ref, left_ref, acc_ref):
+    each = cols // 2
+    acc_ref[:each] = near_ref[:each]
+    add_rows(cols, all_ref, 0, all_ref.shape[0], left_ref, acc_ref, high=each)
+    for c in range(each):
+        panel_ref[c] = (acc_ref[c] * scale_ref[...]).astype(jnp.bfloat16)
+    panel_ref[each:] = sent_ref[each:]
 
 
 def product_kernel(members, n_shot, n_rcv, halves, width, *refs):
@@ -212,7 +219,7 @@
     cols = 2 * per * halves
     block = shots // (n_shot * halves)
     bf16 = functools.partial(jax.ShapeDtypeStruct, dtype=jnp.bfloat16)
-    high, low = dft_tables(window, members, n_rcv, per * halves, main)
+    high, low = dft_tables(window, members, n_rcv, halves, per * halves, main)
 
     message = bf16((n_rows // LANES * (cols + 4), LANES))
     messages = call(
@@ -243,16 +250,18 @@
     tied, acc_near = lax.optimization_barrier((near, acc_near))
     inner = lax.ppermute(tied, SHOT, inner)
     acc_near = call(functools.partial(near_kernel, cols, HEAD, members), acc, (near, acc_near), (left,), flops=NEAR_COST * work)
-    panels = call(
-        functools.partial(far_kernel, cols, halves),
-        (bf16((2 * per + 2, shots, points)),) * halves,
+    panel = bf16((2 * per + 2, shots, points))
+    scratch = (left, pltpu.VMEM(acc.shape, jnp.float32))
+    sent, scale, every = call(
+        functools.partial(far_kernel, cols),
+        (panel, jax.ShapeDtypeStruct((shots, points), jnp.float32), bf16(near.shape)),
         (outer, inner, acc_near, recv_panel[main]),
-        (pltpu.VMEM(near.shape, jnp.bfloat16), left, pltpu.VMEM(acc.shape, jnp.float32), pltpu.VMEM((2, points, lanes), jnp.bfloat16)),
+        scratch + (pltpu.VMEM((2, points, lanes), jnp.bfloat16),),
         flops=FAR_COST * work,
     )
-    panels = list(panels)
-    for k in range(1, halves):
-        panels[k] = lax.ppermute(panels[k], "surf", [(h, h ^ k) for h in range(halves)])
+    came = lax.ppermute(sent, "surf", [(h, h ^ 1) for h in range(halves)])
+    own = call(functools.partial(own_kernel, cols), panel, (every, acc_near, sent, scale), scratch, flops=FAR_COST * work)
+    panels = [own, came]
     out = call(
         functools.partial(product_kernel, members, n_shot, n_rcv, halves, width),
         bf16((n_shot * n_rcv * halves, (2 * per + 1) * block, lanes)),

time: 87 us -> 87.2 us (level)
  waiting for transfers between devices: 4.05 us -> 1.56 us
  Pallas kernels: 28.9 us -> 31.2 us
    pallas_call x6 -> x7, Pallas kernels: 28.9 us -> 31.2 us  [call(): pl.pallas_call(kernel, out_shape=out_shape, in_specs=[VMEM] * len(operand...]
    ppermute x1, waiting for transfers between devices: 1.63 us -> 0.01 us  [local(): came = lax.ppermute(sent, 'surf', [(h, h ^ 1) for h in range(halves)])]
  transfers between devices with their start and end apart: 7 -> 7, of which waited for: 3 -> 2; matrix products, arithmetic and copies ran while one was open for 5% -> 5% of each run, Pallas kernels for 29% -> 31%
where the time goes in v6:
time: 87.2 us; the launch traced here: 86.9 us
  blocking collectives  34.3 us (39%)
  Pallas kernels  31.2 us (36%)
  starting transfers between devices  15.4 us (18%)
  local copies, waits for them, and re-layouts  2.69 us (3%)
  waiting for transfers between devices  1.56 us (2%)
  other arithmetic  1.55 us (2%)
    all_to_all x1, blocking collectives, local(): lax.all_to_all(out, SHOT + ('rcv', 'surf'), split_axis=0, concat_axis=0,...  34.3 us
    pallas_call x7, Pallas kernels, call(): pl.pallas_call(kernel, out_shape=out_shape, in_specs=[VMEM] * len(operand...  31.2 us
    ppermute x1, starting transfers between devices, local(): outer = lax.ppermute(near, SHOT, outer)  5.71 us
    ppermute x3, starting transfers between devices, local(): lax.ppermute(messages[d], 'member', [(t, t ^ d) for t in range(members)])  4.56 us
    all_to_all x1, starting transfers between devices, local(): lax.all_to_all(recv, ('member', 'rcv', 'surf'), split_axis=0, concat_axis...  3.84 us
    dynamic_slice x1, local copies, waits for them, and re-layouts, local(): lax.dynamic_slice_in_dim(recv_panel, start, share, 0)  1.96 us
  transfers between devices with their start and end apart: 7, of which 2 were waited for; matrix products, arithmetic and copies ran while one was open for 5% of the time, Pallas kernels for 31%

profile of v6, /device:TPU:0, one launch (start us, length us, event | category | flops | bytes accessed | tf_op | source)
XLA Modules:
  0.0 86.9 jit_solution(17286088290165106728)
XLA Ops:
  0.0 2.4 %shard_map.73 = (bf16[288,128]{1,0:T(8,128)(2,1)}, bf16[288,128]{1,0:T(8,128)(2,1)}, bf16[288,128]{1,0:T(8,128)(2,1)}, bf16[288,128]{1,0:T(8,128)(2,1)}) custom-call(bf16[1024,256]{1,0:T(8,128)(2,1)} %bitcast.10, bf16[4,4,48,256]{3,2,1,0:T(8,128)(2,1)} %constant.18.clone.high_ref, bf16[4,4,48,256]{3,2,1,0:T(8,128)(2,1)} %constant.19.clone.low_ref, ...), custom_call_target="tpu_custom_call" | custom-call | tf_op jit(solution)/shard_map/pallas_call | solution.py:197
  2.4 4.0 %collective-permute-start = (bf16[288,128]{1,0:T(8,128)(2,1)}, bf16[288,128]{1,0:T(8,128)(2,1)S(1)}, u32[]{:S(2)}, u32[]{:S(2)}) collective-permute-start(bf16[288,128]{1,0:T(8,128)(2,1)} %get-tuple-element.17), channel_id=1, source_target_pairs={{0,12},{4,8},{8,4},{12,0},{1,13},{5,9},{9,5},{13,1},{2,14},{6,10},... | collective-permute-start | bytes 221192 | tf_op jit(solution)/shard_map/ppermute | solution.py:233
  6.3 0.5 collective-permute-start.1
  6.8 0.2 collective-permute-start.2
  6.9 0.7 slice_bitcast_fusion.own_ref
  7.6 2.0 %constant_dynamic-slice_fusion.1 = (bf16[64,2,32,128]{3,2,1,0:T(8,128)(2,1)S(1)}, bf16[64,2,32,128]{3,2,1,0:T(8,128)(2,1)S(1)}) fusion(bf16[129,2,32,128]{3,2,1,0:T(8,128)(2,1)} %param.11, s32[]{:T(128)S(6)} %select_n.6, s32[]{:T(128)S(6)} %select_n.7), kind=kLoop, calls=%fused_computation.4 | loop fusion | bytes 4194312 | tf_op jit(solution)/shard_map/dynamic_slice | solution.py:241
  9.6 0.0 copy-start
  9.6 1.5 %pad_maximum_fusion = bf16[128,2,32,128]{3,2,1,0:T(8,128)(2,1)} fusion(bf16[64,2,32,128]{3,2,1,0:T(8,128)(2,1)S(1)} %get-tuple-element.28, bf16[64,2,32,128]{3,2,1,0:T(8,128)(2,1)S(1)} %get-tuple-element.27), kind=kLoop, calls=%fused_computation | loop fusion | flops 1048576 | bytes 4194304 | tf_op jit(solution)/shard_map/concatenate | solution.py:242
  11.1 0.0 collective-permute-done
  11.1 0.0 collective-permute-done.1
  11.1 0.2 collective-permute-done.2
  11.3 0.0 copy-done
  11.4 5.7 %collective-permute-start.3 = (bf16[4,288,128]{2,1,0:T(8,128)(2,1)S(1)}, bf16[4,288,128]{2,1,0:T(8,128)(2,1)S(1)}, u32[]{:S(2)}, u32[]{:S(2)}) collective-permute-start(bf16[4,288,128]{2,1,0:T(8,128)(2,1)S(1)} %pad_maximum_fusion.1.rows_ref), channel_id=1, source_target_pairs={{0,24},{4,28},{24,0},{28,4},{1,25},{5,29},{25,1},{29,5},{2,26},{6,... | collective-permute-start | bytes 884744 | tf_op jit(solution)/shard_map/ppermute | solution.py:237
  17.1 3.8 %all-to-all-start = ((bf16[16,512,128]{2,1,0:T(8,128)(2,1)}), bf16[16,512,128]{2,1,0:T(8,128)(2,1)S(1)}, u32[]{:S(2)}, u32[]{:S(2)}) async-start(bf16[16,512,128]{2,1,0:T(8,128)(2,1)} %bitcast.9), calls=%async_computation | async-start | bytes 4194304 | tf_op jit(solution)/shard_map/all_to_all | solution.py:244
  20.9 3.0 %shard_map.74.refs_0_ = f32[35,128,128]{2,1,0:T(8,128)S(1)} custom-call(bf16[4,288,128]{2,1,0:T(8,128)(2,1)S(1)} %pad_maximum_fusion.1.rows_ref), custom_call_target="tpu_custom_call" | custom-call | flops 28185722880 | tf_op jit(solution)/shard_map/pallas_call | solution.py:197
  23.9 0.9 collective-permute-start.4
  24.8 9.3 %shard_map.75.near_ref = f32[35,128,128]{2,1,0:T(8,128)S(1)} custom-call(bf16[4,288,128]{2,1,0:T(8,128)(2,1)S(1)} %pad_maximum_fusion.1.rows_ref, f32[35,128,128]{2,1,0:T(8,128)S(1)} %shard_map.74.refs_0_), custom_call_target="tpu_custom_call" | custom-call | flops 14092861440 | tf_op jit(solution)/shard_map/pallas_call | solution.py:197
  34.1 0.0 collective-permute-done.4.inner_ref
  34.1 0.0 collective-permute-done.3.outer_ref
  34.1 8.1 %shard_map.76 = (bf16[18,128,128]{2,1,0:T(8,128)(2,1)S(1)}, f32[128,128]{1,0:T(8,128)S(1)}, bf16[4,288,128]{2,1,0:T(8,128)(2,1)S(1)}) custom-call(bf16[4,288,128]{2,1,0:T(8,128)(2,1)S(1)} %collective-permute-done.3.outer_ref, bf16[4,288,128]{2,1,0:T(8,128)(2,1)S(1)} %collective-permute-done.4.inner_ref, f32[35,128,128]{2,1,0:T(8,128)S(1)} %shard_map.75.near_ref, ...), custom_call_target="tpu_custom_call" | custom-call | flops 7046430720 | tf_op jit(solution)/shard_map/pallas_call | solution.py:197
  42.2 0.5 collective-permute-start.5
  42.7 6.9 %shard_map.77.refs_0_ = bf16[18,128,128]{2,1,0:T(8,128)(2,1)S(1)} custom-call(bf16[4,288,128]{2,1,0:T(8,128)(2,1)S(1)} %get-tuple-element.23.all_ref, f32[35,128,128]{2,1,0:T(8,128)S(1)} %shard_map.75.near_ref, bf16[18,128,128]{2,1,0:T(8,128)(2,1)S(1)} %get-tuple-element.24.sent_ref, f32[128,128]{1,0:T(8,128)S(1)} %get-tuple-element.25.scale_ref), custom_call_target="tpu_custom_call" | custom-call | flops 7046430720 | tf_op jit(solution)/shard_map/pallas_call | solution.py:197
  49.5 0.0 collective-permute-done.5.refs_1_
  49.6 1.4 %all-to-all-done.refs_2_ = bf16[16,512,128]{2,1,0:T(8,128)(2,1)S(1)} async-done(((bf16[16,512,128]{2,1,0:T(8,128)(2,1)}), bf16[16,512,128]{2,1,0:T(8,128)(2,1)S(1)}, u32[]{:S(2)}, u32[]{:S(2)}) %all-to-all-start) | async-done | bytes 2097184 | tf_op jit(solution)/shard_map/all_to_all | solution.py:244
  50.9 0.7 shard_map.78
  51.6 34.3 %all_to_all.10.got_ref = bf16[32,136,128]{2,1,0:T(8,128)(2,1)S(1)} all-to-all(bf16[32,136,128]{2,1,0:T(8,128)(2,1)S(1)} %shard_map.78), channel_id=1, replica_groups=mesh['group'=2,'member'=4,'rcv'=2,'surf'=2] {'group','member','rcv','surf'}, dimensions={0} | all-to-all | bytes 2228224 | tf_op jit(solution)/shard_map/all_to_all | solution.py:270
  86.0 0.9 %shard_map.79 = bf16[129,2,8,128]{3,2,1,0:T(8,128)(2,1)} custom-call(bf16[32,136,128]{2,1,0:T(8,128)(2,1)S(1)} %all_to_all.10.got_ref), custom_call_target="tpu_custom_call" | custom-call | tf_op jit(solution)/shard_map/pallas_call | solution.py:197
  (1 shorter events, 0.0 us)
Async XLA Ops:
  2.4 8.8 %collective-permute-start = (bf16[288,128]{1,0:T(8,128)(2,1)}, bf16[288,128]{1,0:T(8,128)(2,1)S(1)}, u32[]{:S(2)}, u32[]{:S(2)}) collective-permute-start(bf16[288,128]{1,0:T(8,128)(2,1)} %get-tuple-element.17), channel_id=1, source_target_pairs={{0,12},{4,8},{8,4},{12,0},{1,13},{5,9},{9,5},{13,1},{2,14},{6,10},... | collective-permute-start | bytes 221192 | tf_op jit(solution)/shard_map/ppermute | solution.py:233
  6.3 4.8 %collective-permute-start.1 = (bf16[288,128]{1,0:T(8,128)(2,1)}, bf16[288,128]{1,0:T(8,128)(2,1)S(1)}, u32[]{:S(2)}, u32[]{:S(2)}) collective-permute-start(bf16[288,128]{1,0:T(8,128)(2,1)} %get-tuple-element.18), channel_id=1, source_target_pairs={{0,8},{4,12},{8,0},{12,4},{1,9},{5,13},{9,1},{13,5},{2,10},{6,14},... | collective-permute-start | bytes 221192 | tf_op jit(solution)/shard_map/ppermute | solution.py:233
  6.8 4.6 %collective-permute-start.2 = (bf16[288,128]{1,0:T(8,128)(2,1)}, bf16[288,128]{1,0:T(8,128)(2,1)S(1)}, u32[]{:S(2)}, u32[]{:S(2)}) collective-permute-start(bf16[288,128]{1,0:T(8,128)(2,1)} %get-tuple-element.19), channel_id=1, source_target_pairs={{0,4},{4,0},{8,12},{12,8},{1,5},{5,1},{9,13},{13,9},{2,6},{6,2},{1... | collective-permute-start | bytes 221192 | tf_op jit(solution)/shard_map/ppermute | solution.py:233
  9.6 1.7 %copy-start = (bf16[288,128]{1,0:T(8,128)(2,1)S(1)}, bf16[288,128]{1,0:T(8,128)(2,1)}, u32[]{:S(2)}) copy-start(bf16[288,128]{1,0:T(8,128)(2,1)} %get-tuple-element.16) | copy-start | bytes 221188
  11.4 22.7 %collective-permute-start.3 = (bf16[4,288,128]{2,1,0:T(8,128)(2,1)S(1)}, bf16[4,288,128]{2,1,0:T(8,128)(2,1)S(1)}, u32[]{:S(2)}, u32[]{:S(2)}) collective-permute-start(bf16[4,288,128]{2,1,0:T(8,128)(2,1)S(1)} %pad_maximum_fusion.1.rows_ref), channel_id=1, source_target_pairs={{0,24},{4,28},{24,0},{28,4},{1,25},{5,29},{25,1},{29,5},{2,26},{6,... | collective-permute-start | bytes 884744 | tf_op jit(solution)/shard_map/ppermute | solution.py:237
  17.1 33.8 %all-to-all-start = ((bf16[16,512,128]{2,1,0:T(8,128)(2,1)}), bf16[16,512,128]{2,1,0:T(8,128)(2,1)S(1)}, u32[]{:S(2)}, u32[]{:S(2)}) async-start(bf16[16,512,128]{2,1,0:T(8,128)(2,1)} %bitcast.9), calls=%async_computation | async-start | bytes 4194304 | tf_op jit(solution)/shard_map/all_to_all | solution.py:244
  23.9 10.1 %collective-permute-start.4 = (bf16[4,288,128]{2,1,0:T(8,128)(2,1)S(1)}, bf16[4,288,128]{2,1,0:T(8,128)(2,1)S(1)}, u32[]{:S(2)}, u32[]{:S(2)}) collective-permute-start(bf16[4,288,128]{2,1,0:T(8,128)(2,1)S(1)} %pad_maximum_fusion.1.rows_ref), channel_id=1, source_target_pairs={{8,16},{12,20},{16,8},{20,12},{9,17},{13,21},{17,9},{21,13},{10,18... | collective-permute-start | bytes 884744 | tf_op jit(solution)/shard_map/ppermute | solution.py:251
  42.2 7.3 %collective-permute-start.5 = (bf16[18,128,128]{2,1,0:T(8,128)(2,1)S(1)}, bf16[18,128,128]{2,1,0:T(8,128)(2,1)S(1)}, u32[]{:S(2)}, u32[]{:S(2)}) collective-permute-start(bf16[18,128,128]{2,1,0:T(8,128)(2,1)S(1)} %get-tuple-element.24.sent_ref), channel_id=1, source_target_pairs={{0,1},{1,0},{2,3},{3,2},{4,5},{5,4},{6,7},{7,6},{8,9},{9,8},{10,11... | collective-permute-start | bytes 1769480 | tf_op jit(solution)/shard_map/ppermute | solution.py:262
